TPU v7x, 256 devices: a whole 4x4x8 slice. The times are simulated.
256 devices in a mesh: sky: 32 (over z, x), exp: 8 (over y, core).
Axes of the slice: x: 4, y: 4, z: 8, core: 2. Of those that a mesh axis runs over, the one named last changes fastest.
Arguments:
- image: float32 [64, 1024, 2048], P('exp', 'sky'), may hold values from -6 to 6
- variance: float32 [64, 1024, 2048], P('exp', 'sky'), may hold values from 0.25 to 4
- coef_index: int32 [64], P('exp'), may hold values from 0 to 15
- coef_table: float32 [16, 5], replicated, may hold values from -3 to 3
- row_taps: float32 [5, 41], replicated, may hold values from -1 to 1
- col_taps: float32 [5, 41], replicated, may hold values from -1 to 1
- destination: int32 [8, 32, 64, 1], P('exp', 'sky'), may hold values from 0 to 31; in each aligned block of 64 rows (0 to 63, 64 to 127, ..., all dimensions but the last counted through in order) at most 4 rows name the same one
- offset: int32 [8, 32, 64], P('exp', 'sky'), may hold values from 0 to 120
Outputs:
- coadd: float32 [4096, 1024], P(('sky', 'exp'))
- weight_map: float32 [4096, 1024], P(('sky', 'exp'))
Inputs may be any that keep to these rules, and one draw needn't show every extreme that they name: `destination`: among the strips of one device no patch is named more than 4 times, and some device names some patch exactly 4 times.
All inputs are finite; a program needn't handle non-finite values.
Results may differ from a plain program's by a relative error of at most 0.000082.
Values sent between devices are 32-bit elements; how exact they have to be, the bound alone decides.
A program may use at most 128 MiB of HBM per device.

v0:
```python
import jax
import jax.numpy as jnp
from jax import lax
from jax.sharding import PartitionSpec as P

SR = 8
PR = 128


def extended(cells, sides, width):
    for axis, dim in sides:
        count = lax.axis_size(axis)
        ends = count - 1
        head = lax.slice_in_dim(cells, 0, width, axis=dim)
        tail = lax.slice_in_dim(cells, cells.shape[dim] - width, cells.shape[dim], axis=dim)
        cells = jnp.concatenate(
            [
                lax.ppermute(tail, axis, [(i, (i + 1) % count) for i in range(ends)]),
                cells,
                lax.ppermute(head, axis, [((i + 1) % count, i) for i in range(ends)]),
            ],
            axis=dim,
        )
    return cells


def per_device(image, variance, coef_index, coef_table, row_taps, col_taps, destination, offset):
    highest = lax.Precision.HIGHEST
    basis_count, tap_count = row_taps.shape
    rim_rows = (tap_count - 1) // 2
    exp_count, tile_rows, tile_cols = image.shape
    half_cols = tile_cols // 2
    block_cols = 128
    col_blocks = tile_cols // block_cols
    padded = extended(image, (("sky", 1),), rim_rows)
    chosen = (
        coef_index[:, None] == jnp.arange(coef_table.shape[0], dtype=jnp.int32)[None, :]
    ).astype(jnp.float32)
    coefficients = jnp.dot(chosen, coef_table, precision=highest)
    row_lag = (
        jnp.arange(tile_rows + 2 * rim_rows, dtype=jnp.int32)[None, :]
        - jnp.arange(tile_rows, dtype=jnp.int32)[:, None]
    )
    col_lag = (
        jnp.arange(3 * block_cols, dtype=jnp.int32)[:, None]
        - jnp.arange(block_cols, dtype=jnp.int32)[None, :]
        + rim_rows
        - block_cols
    )
    tap_ids = jnp.arange(tap_count, dtype=jnp.int32)
    matched = jnp.zeros((exp_count, tile_rows, tile_cols), jnp.float32)
    for basis_idx in range(basis_count):
        vertical = jnp.sum(jnp.where(row_lag[:, :, None] == tap_ids, row_taps[basis_idx], 0.0), -1)
        horizontal = jnp.sum(
            jnp.where(col_lag[:, :, None] == tap_ids, col_taps[basis_idx], 0.0), -1
        )
        across = jnp.einsum("yk,ekx->eyx", vertical, padded, precision=highest)
        spread = jnp.pad(across, ((0, 0), (0, 0), (block_cols, block_cols))).reshape(
            exp_count, tile_rows, col_blocks + 2, block_cols
        )
        window = jnp.concatenate([spread[:, :, :-2], spread[:, :, 1:-1], spread[:, :, 2:]], -1)
        basis_term = jnp.einsum("eykw,wu->eyku", window, horizontal, precision=highest).reshape(
            exp_count, tile_rows, tile_cols
        )
        matched = matched + coefficients[:, basis_idx][:, None, None] * basis_term
    weight = 1.0 / variance
    weighted = weight * matched

    def to_strips(field):
        shaped = field.reshape(exp_count, tile_rows // SR, SR, 2, half_cols)
        return shaped.transpose(0, 1, 3, 2, 4).reshape(-1, SR, half_cols)

    payload = jnp.stack([to_strips(weighted), to_strips(weight)], 2)
    strip_count = payload.shape[0]
    sky_count = lax.axis_size("sky")
    targets_patch = destination.reshape(-1)
    row_offsets = offset.reshape(-1)
    payload = payload.reshape(strip_count, SR * 2 * half_cols)
    capacity = max(2, 2 * strip_count // sky_count)
    member = (targets_patch[:, None] == jnp.arange(sky_count, dtype=jnp.int32)[None, :]).astype(
        jnp.int32
    )
    slot_rank = jnp.sum((jnp.cumsum(member, 0) - member) * member, 1)
    slot_index = targets_patch * capacity + slot_rank
    selector = slot_index[None, :] == jnp.arange(sky_count * capacity, dtype=jnp.int32)[:, None]
    packed = jnp.dot(selector.astype(jnp.float32), payload, precision=highest).reshape(
        sky_count, capacity, SR * 2 * half_cols
    )
    placed_offsets = jnp.sum(jnp.where(selector, row_offsets[None, :], 0), 1).reshape(
        sky_count, capacity
    )
    received, received_offsets = (
        lax.all_to_all(packed, "sky", split_axis=0, concat_axis=0, tiled=True),
        lax.all_to_all(placed_offsets, "sky", split_axis=0, concat_axis=0, tiled=True),
    )
    target_rows = (
        received_offsets.reshape(-1)[:, None] + jnp.arange(SR, dtype=jnp.int32)[None, :]
    ).reshape(-1)
    placement = (target_rows[None, :] == jnp.arange(PR, dtype=jnp.int32)[:, None]).astype(
        jnp.float32
    )
    partial_value = jnp.dot(placement, received.reshape(-1, 2 * half_cols), precision=highest)
    summed = lax.psum_scatter(partial_value, "exp", scatter_dimension=0, tiled=True)
    weighted_sum = summed[:, :half_cols]
    weight_map = summed[:, half_cols:]
    coadd = weighted_sum / (1.0 + weight_map)
    return (coadd, weight_map)


def solution(mesh):
    placed = (
        P("exp", "sky", None),
        P("exp", "sky", None),
        P("exp"),
        P(),
        P(),
        P(),
        P("exp", "sky", None, None),
        P("exp", "sky", None),
    )
    return jax.shard_map(
        per_device,
        mesh=mesh,
        in_specs=placed,
        out_specs=(P(("sky", "exp"), None), P(("sky", "exp"), None)),
        check_vma=False,
    )
```

profile of v0, /device:TPU:4, one launch (start us, length us, event | category | flops | bytes accessed | tf_op | source)
XLA Modules:
  0.0 478.4 jit_solution(2258280249932627505)
XLA Ops:
  19.3 12.5 %all-to-all-start = ((s32[32,1,4]{2,1,0:T(1,128)}), s32[32,1,4]{2,1,0:T(1,128)}, u32[]{:S(2)}, u32[]{:S(2)}) async-start(s32[32,1,4]{2,1,0:T(1,128)} %bitcast.2), calls=%async_computation | async-start | bytes 32768 | tf_op jit(solution)/shard_map/all_to_all | solution.py:94
  33.0 4.6 select_reduce_fusion.4
  37.6 5.3 %collective-permute-done = f32[8,20,2048]{2,0,1:T(8,128)S(1)} collective-permute-done((f32[8,20,2048]{2,0,1:T(8,128)S(1)}, f32[8,20,2048]{2,0,1:T(8,128)S(1)}, u32[]{:S(2)}, u32[]{:S(2)}) %collective-permute-start) | collective-permute-done | bytes 1310752 | tf_op jit(solution)/shard_map/ppermute | solution.py:18
  43.7 4.2 collective-permute-done.1
  55.1 3.8 reshape.130
  58.9 4.3 fusion.54
  63.1 6.7 %fusion = f32[8,32,16,128]{3,2,1,0:T(8,128)} fusion(f32[8,32,16,128]{3,2,1,0:T(8,128)S(1)} %get-tuple-element.15, f32[8,32,16,128]{3,2,1,0:T(8,128)S(1)} %get-tuple-element.16, f32[8,32,16,128]{3,2,1,0:T(8,128)S(1)} %get-tuple-element.14, f32[384,128]{1,0:T(8,128)S(1)} %copy-done.5), kind=kOutput, calls=%fused_computation.6 | convolution fusion | flops 2419064832 | bytes 8585216 | tf_op jit(solution)/shard_map/eykw,wu->eyku/dot_general | solution.py:62
  72.6 5.0 %convolution_bitcast_fusion.3 = f32[8,32,2048]{2,1,0:T(8,128)S(1)} fusion(f32[32,72]{1,0:T(8,128)S(1)} %get-tuple-element.11, f32[8,20,2048]{2,1,0:T(8,128)} %copy-done.4, f32[8,32,2048]{2,1,0:T(8,128)S(1)} %copy-done.2, f32[8,20,2048]{2,1,0:T(8,128)} %copy-done.3), kind=kOutput, calls=%fused_computation.41 | convolution fusion | flops 455344128 | bytes 6824960 | tf_op jit(solution)/shard_map/yk,ekx->eyx/dot_general | solution.py:57
  79.2 3.8 reshape.132
  83.0 4.2 fusion.55
  87.2 6.7 %fusion.6 = f32[8,32,16,128]{3,2,1,0:T(8,128)} fusion(f32[8,32,16,128]{3,2,1,0:T(8,128)S(1)} %get-tuple-element.18, f32[8,32,16,128]{3,2,1,0:T(8,128)S(1)} %get-tuple-element.19, f32[8,32,16,128]{3,2,1,0:T(8,128)S(1)} %get-tuple-element.17, f32[384,128]{1,0:T(8,128)S(1)} %get-tuple-element.6), kind=kOutput, calls=%fused_computation.12 | convolution fusion | flops 2419064832 | bytes 8585216 | tf_op jit(solution)/shard_map/eykw,wu->eyku/dot_general | solution.py:62
  96.7 5.0 %convolution_bitcast_fusion.2 = f32[8,32,2048]{2,1,0:T(8,128)S(1)} fusion(f32[32,72]{1,0:T(8,128)S(1)} %get-tuple-element.10, f32[8,20,2048]{2,1,0:T(8,128)} %copy-done.4, f32[8,32,2048]{2,1,0:T(8,128)S(1)} %copy-done.2, f32[8,20,2048]{2,1,0:T(8,128)} %copy-done.3), kind=kOutput, calls=%fused_computation.40 | convolution fusion | flops 455344128 | bytes 6824960 | tf_op jit(solution)/shard_map/yk,ekx->eyx/dot_general | solution.py:57
  103.3 3.9 reshape.134
  107.2 4.2 fusion.56
  111.4 6.7 %fusion.12 = f32[8,32,16,128]{3,2,1,0:T(8,128)} fusion(f32[8,32,16,128]{3,2,1,0:T(8,128)S(1)} %get-tuple-element.21, f32[8,32,16,128]{3,2,1,0:T(8,128)S(1)} %get-tuple-element.22, f32[8,32,16,128]{3,2,1,0:T(8,128)S(1)} %get-tuple-element.20, f32[384,128]{1,0:T(8,128)S(1)} %get-tuple-element.5), kind=kOutput, calls=%fused_computation.18 | convolution fusion | flops 2419064832 | bytes 8585216 | tf_op jit(solution)/shard_map/eykw,wu->eyku/dot_general | solution.py:62
  120.8 5.0 %convolution_bitcast_fusion.1 = f32[8,32,2048]{2,1,0:T(8,128)S(1)} fusion(f32[32,72]{1,0:T(8,128)S(1)} %get-tuple-element.9, f32[8,20,2048]{2,1,0:T(8,128)} %copy-done.4, f32[8,32,2048]{2,1,0:T(8,128)S(1)} %copy-done.2, f32[8,20,2048]{2,1,0:T(8,128)} %copy-done.3), kind=kOutput, calls=%fused_computation.39 | convolution fusion | flops 455344128 | bytes 6824960 | tf_op jit(solution)/shard_map/yk,ekx->eyx/dot_general | solution.py:57
  127.4 4.1 reshape.136
  131.5 4.2 fusion.57
  135.8 6.7 %fusion.18 = f32[8,32,16,128]{3,2,1,0:T(8,128)} fusion(f32[8,32,16,128]{3,2,1,0:T(8,128)S(1)} %get-tuple-element.24, f32[8,32,16,128]{3,2,1,0:T(8,128)S(1)} %get-tuple-element.25, f32[8,32,16,128]{3,2,1,0:T(8,128)S(1)} %get-tuple-element.23, f32[384,128]{1,0:T(8,128)S(1)} %get-tuple-element.4), kind=kOutput, calls=%fused_computation.24 | convolution fusion | flops 2419064832 | bytes 8585216 | tf_op jit(solution)/shard_map/eykw,wu->eyku/dot_general | solution.py:62
  145.1 5.0 %convolution_bitcast_fusion = f32[8,32,2048]{2,1,0:T(8,128)S(1)} fusion(f32[32,72]{1,0:T(8,128)S(1)} %get-tuple-element.8, f32[8,20,2048]{2,1,0:T(8,128)} %copy-done.4, f32[8,32,2048]{2,1,0:T(8,128)S(1)} %copy-done.2, f32[8,20,2048]{2,1,0:T(8,128)} %copy-done.3), kind=kOutput, calls=%fused_computation.38 | convolution fusion | flops 455344128 | bytes 6824960 | tf_op jit(solution)/shard_map/yk,ekx->eyx/dot_general | solution.py:57
  155.0 5.8 %fusion.24 = f32[8,32,16,128]{3,2,1,0:T(8,128)S(1)} fusion(f32[8,32,16,128]{3,2,1,0:T(8,128)S(1)} %get-tuple-element.27, f32[8,32,16,128]{3,2,1,0:T(8,128)S(1)} %get-tuple-element.28, f32[8,32,16,128]{3,2,1,0:T(8,128)S(1)} %get-tuple-element.26, f32[384,128]{1,0:T(8,128)S(1)} %get-tuple-element.3), kind=kOutput, calls=%fused_computation.30 | convolution fusion | flops 2419064832 | bytes 8585216 | tf_op jit(solution)/shard_map/eykw,wu->eyku/dot_general | solution.py:62
  162.4 8.6 %add_multiply_fusion = (f32[8,32,2048]{2,1,0:T(8,128)}, f32[8,32,2048]{2,1,0:T(8,128)}) fusion(f32[8,32,2048]{2,1,0:T(8,128)} %reshape.139, f32[8,32,2048]{2,1,0:T(8,128)} %reshape.137, f32[8,32,2048]{2,1,0:T(8,128)} %reshape.135, f32[8,32,2048]{2,1,0:T(8,128)} %reshape.133, f32[8,32,2048]{2,1,0:T(8,128)} %reshape.131, f32[8]{0:T(128)S(1)} %get-tuple-element.34, ...), kind=kLoop, calls=%fused_computation.43 | loop fusion | flops 5767168 | bytes 16777376 | tf_op jit(solution)/shard_map/mul | solution.py:67
  174.8 4.9 %stack_reshape.7 = f32[64,8,1,1024]{3,2,1,0:T(1,128)} reshape(f32[8,4,2,8,1024]{4,3,2,1,0:T(8,128)} %bitcast.107) | data formatting | bytes 4194304 | tf_op jit(solution)/shard_map/stack;reshape | solution.py:73
  179.7 7.8 %pad_maximum_fusion.1 = f32[64,8,2,1024]{3,2,1,0:T(2,128)} fusion(f32[64,8,1,1024]{3,2,1,0:T(1,128)} %stack_reshape.7, f32[64,8,1,1024]{3,2,1,0:T(1,128)S(1)} %stack_reshape.6), kind=kLoop, calls=%fused_computation.37 | loop fusion | flops 1048576 | bytes 8388608 | tf_op jit(solution)/shard_map/stack | solution.py:73
  187.5 6.6 %reshape.154 = f32[64,16384,1]{1,0,2:T(8,128)} reshape(f32[64,8,2,1024]{3,2,1,0:T(2,128)} %pad_maximum_fusion.1) | data formatting | bytes 8388608 | tf_op jit(solution)/shard_map/reshape | solution.py:78
  194.1 9.0 %fusion.37 = f32[32,4,16384]{2,0,1:T(8,128)} fusion(f32[64,16384,1]{1,0,2:T(8,128)} %reshape.154, s32[32,4]{0,1:T(4,128)S(1)} %multiply_add_fusion, s32[64]{0:T(128)S(1)} %copy-done.12), kind=kOutput, calls=%fused_computation.62 | convolution fusion | flops 1610620928 | bytes 12583680 | tf_op jit(solution)/shard_map/dot_general | solution.py:86
  203.1 12.0 %copy.22 = f32[32,4,16384]{2,1,0:T(4,128)} copy(f32[32,4,16384]{2,0,1:T(8,128)} %fusion.37) | data formatting | bytes 16777216 | tf_op jit(solution)/shard_map/dot_general | solution.py:86
  215.1 14.1 %all-to-all-start.1 = ((f32[32,4,16384]{2,1,0:T(4,128)}), f32[32,4,16384]{2,1,0:T(4,128)}, u32[]{:S(2)}, u32[]{:S(2)}) async-start(f32[32,4,16384]{2,1,0:T(4,128)} %copy.22), calls=%async_computation.1 | async-start | bytes 16777216 | tf_op jit(solution)/shard_map/all_to_all | solution.py:93
  231.5 177.2 %all-to-all-done.1 = f32[32,4,16384]{2,1,0:T(4,128)} async-done(((f32[32,4,16384]{2,1,0:T(4,128)}), f32[32,4,16384]{2,1,0:T(4,128)}, u32[]{:S(2)}, u32[]{:S(2)}) %all-to-all-start.1) | async-done | bytes 8388640 | tf_op jit(solution)/shard_map/all_to_all | solution.py:93
  408.6 10.9 %reshape.143 = f32[1024,2048]{1,0:T(8,128)} reshape(f32[32,4,16384]{2,1,0:T(4,128)} %all-to-all-done.1) | data formatting | bytes 16777216 | tf_op jit(solution)/shard_map/reshape | solution.py:102
  419.5 7.6 %fusion.30 = f32[128,2048]{1,0:T(8,128)} fusion(f32[1024,2048]{1,0:T(8,128)} %reshape.143, s32[1024]{0:T(1024)S(1)} %add.78), kind=kOutput, calls=%fused_computation.52 | convolution fusion | flops 3221356544 | bytes 9441280 | tf_op jit(solution)/shard_map/dot_general | solution.py:102
  427.1 42.4 %reduce-scatter.2.cloned.1.call-done = f32[16,2048]{1,0:T(8,128)} async-done(((f32[128,2048]{1,0:T(8,128)}), f32[16,2048]{1,0:T(8,128)}) %reduce-scatter.2.cloned.1.call-update) | async-done | bytes 131088 | tf_op jit(solution)/shard_map/reduce_scatter | solution.py:103
  (74 shorter events, 50.9 us)
Async XLA Ops:
  7.2 24.7 %copy-start = (f32[16,5]{0,1:T(8,128)S(1)}, f32[16,5]{0,1:T(8,128)}, u32[]{:S(2)}) copy-start(f32[16,5]{0,1:T(8,128)} %param.11) | copy-start | bytes 964
  10.2 7.9 %copy-start.6 = (s32[1,1,64,1]{2,3,1,0:T(1,128)S(1)}, s32[1,1,64,1]{2,3,1,0:T(1,128)}, u32[]{:S(2)}) copy-start(s32[1,1,64,1]{2,3,1,0:T(1,128)} %param.14) | copy-start | bytes 772
  10.2 8.2 %copy-start.13 = (s32[1,1,64]{2,1,0:T(1,128)S(1)}, s32[1,1,64]{2,1,0:T(1,128)}, u32[]{:S(2)}) copy-start(s32[1,1,64]{2,1,0:T(1,128)} %param.15) | copy-start | bytes 772
  10.2 21.6 %copy-start.9 = (f32[5,41]{1,0:T(8,128)S(1)}, f32[5,41]{1,0:T(8,128)}, u32[]{:S(2)}) copy-start(f32[5,41]{1,0:T(8,128)} %param.12) | copy-start | bytes 2464
  10.2 21.6 %copy-start.10 = (f32[5,41]{1,0:T(8,128)S(1)}, f32[5,41]{1,0:T(8,128)}, u32[]{:S(2)}) copy-start(f32[5,41]{1,0:T(8,128)} %param.13) | copy-start | bytes 2464
  10.2 21.6 %copy-start.14 = (s32[8]{0:T(128)S(1)}, s32[8]{0:T(128)}, u32[]{:S(2)}) copy-start(s32[8]{0:T(128)} %param.10) | copy-start | bytes 100
  10.2 32.7 %collective-permute-start = (f32[8,20,2048]{2,0,1:T(8,128)S(1)}, f32[8,20,2048]{2,0,1:T(8,128)S(1)}, u32[]{:S(2)}, u32[]{:S(2)}) collective-permute-start(f32[8,20,2048]{2,0,1:T(8,128)S(1)} %copy.28), channel_id=1, source_target_pairs={{0,8},{8,16},{16,24},{24,32},{32,40},{40,48},{48,56},{56,64},{64,7... | collective-permute-start | bytes 3932168 | tf_op jit(solution)/shard_map/ppermute | solution.py:18
  15.3 32.6 %collective-permute-start.1 = (f32[8,20,2048]{2,0,1:T(8,128)}, f32[8,20,2048]{2,0,1:T(8,128)}, u32[]{:S(2)}, u32[]{:S(2)}) collective-permute-start(f32[8,20,2048]{2,0,1:T(8,128)} %copy.29), channel_id=1, source_target_pairs={{8,0},{16,8},{24,16},{32,24},{40,32},{48,40},{56,48},{64,56},{72,6... | collective-permute-start | bytes 3932168 | tf_op jit(solution)/shard_map/ppermute | solution.py:20
  18.4 0.8 copy-start.11
  19.3 195.8 %all-to-all-start = ((s32[32,1,4]{2,1,0:T(1,128)}), s32[32,1,4]{2,1,0:T(1,128)}, u32[]{:S(2)}, u32[]{:S(2)}) async-start(s32[32,1,4]{2,1,0:T(1,128)} %bitcast.2), calls=%async_computation | async-start | bytes 32768 | tf_op jit(solution)/shard_map/all_to_all | solution.py:94
  43.7 9.7 %copy-start.3 = (f32[8,20,2048]{2,1,0:T(8,128)}, f32[8,20,2048]{2,1,0:T(8,128)S(1)}, u32[]{:S(2)}) copy-start(f32[8,20,2048]{2,1,0:T(8,128)S(1)} %copy.20) | copy-start | bytes 3932164
  43.7 6.4 %copy-start.2 = (f32[8,32,2048]{2,1,0:T(8,128)S(1)}, f32[8,32,2048]{2,1,0:T(8,128)}, u32[]{:S(2)}) copy-start(f32[8,32,2048]{2,1,0:T(8,128)} %param.8) | copy-start | bytes 6291460
  50.0 3.3 copy-start.4
  58.9 4.3 copy-start.5
  160.8 1.6 copy-start.7
  160.8 1.5 copy-start.8
  187.5 6.6 %copy-start.12 = (s32[64]{0:T(128)S(1)}, s32[64]{0:T(128)}, u32[]{:S(2)}) copy-start(s32[64]{0:T(128)} %copy-done.11) | copy-start | bytes 772
  215.1 193.5 %all-to-all-start.1 = ((f32[32,4,16384]{2,1,0:T(4,128)}), f32[32,4,16384]{2,1,0:T(4,128)}, u32[]{:S(2)}, u32[]{:S(2)}) async-start(f32[32,4,16384]{2,1,0:T(4,128)} %copy.22), calls=%async_computation.1 | async-start | bytes 16777216 | tf_op jit(solution)/shard_map/all_to_all | solution.py:93
  229.2 240.3 %reduce-scatter.2.cloned.1.call-start = ((), (), s32[]{:S(2)}) async-start(), calls=%async_computation.3 | async-start | bytes 1179648 | tf_op jit(solution)/shard_map/reduce_scatter | solution.py:103
  419.5 51.6 %copy-start.1 = (f32[16,5]{0,1:T(8,128)S(1)}, f32[16,5]{0,1:T(8,128)}, u32[]{:S(2)}) copy-start(f32[16,5]{0,1:T(8,128)} %param.11) | copy-start | bytes 964
Sparse Core Ops, SparseCore 0:
  427.2 42.2 reduce-scatter.1
where the time goes:
time: 487 us; the launch traced here: 478 us
  waiting for transfers between devices  229 us (47%)
  local copies, waits for them, and re-layouts  104 us (21%)
  matrix products  72.4 us (15%)
  starting transfers between devices  32.6 us (7%)
  other arithmetic  25 us (5%)
  between operations  14.9 us (3%)
    all_to_all x1, waiting for transfers between devices, per_device(): lax.all_to_all(packed, 'sky', split_axis=0, concat_axis=0, tiled=True)  177 us
    reduce_scatter x1, waiting for transfers between devices, per_device(): lax.psum_scatter(partial_value, 'exp', scatter_dimension=0, tiled=True)  42.4 us
    dot_general x5, matrix products, per_device(): jnp.einsum('eykw,wu->eyku', window, horizontal, precision=highest)  32.5 us
    dot_general x5, matrix products, per_device(): across = jnp.einsum('yk,ekx->eyx', vertical, padded, precision=highest)  23.1 us
    reshape x5, local copies, waits for them, and re-layouts, per_device(): jnp.pad(across, ((0, 0), (0, 0), (block_cols, block_cols)))  18.2 us
    slice x5, local copies, waits for them, and re-layouts, per_device(): spread[:, :, :-2]  17.6 us
    all_to_all x1, starting transfers between devices, per_device(): lax.all_to_all(packed, 'sky', split_axis=0, concat_axis=0, tiled=True)  14.1 us
    all_to_all x1, starting transfers between devices, per_device(): lax.all_to_all(placed_offsets, 'sky', split_axis=0, concat_axis=0, tiled=...  12.5 us
  transfers between devices with their start and end apart: 5, of which 4 were waited for; matrix products, arithmetic and copies ran while one was open for 37% of the time, Pallas kernels for 0%

commit v1 on v0

v1 whole, which is shorter than its diff:
```python
import jax
import jax.numpy as jnp
from jax import lax
from jax.experimental import pallas as pl
from jax.experimental.pallas import tpu as pltpu
from jax.sharding import PartitionSpec as P

MESH = pl.DeviceIdType.MESH
F32, BF16, I32 = jnp.float32, jnp.bfloat16, jnp.int32

NB, TAPS, RIM = 5, 41, 20
N_SKY, N_EXP, NX, NZ = 32, 8, 4, 8
EXPS, ROWS, COLS, HALF = 8, 32, 2048, 1024
BLOCKS = EXPS * ROWS // 8
LANES = 128
PR, PATCH_ROWS = 128, 4096
PER = 4
CHUNKS = EXPS // PER
STEP = 256
NSTEP = COLS // STEP


def iota(shape, dim):
    return lax.broadcasted_iota(I32, shape, dim)


def greet(devices):
    barrier = pltpu.get_barrier_semaphore()
    for device in devices:
        pl.semaphore_signal(barrier, inc=1, device_id=device, device_id_type=MESH)
    pl.semaphore_wait(barrier, len(devices))


def split(value):
    high = value.astype(BF16)
    return high, (value - high.astype(F32)).astype(BF16)


def match_kernel(
    image, variance, dest, offs, coef_index, coef_table, row_taps, col_taps,
    out_w, out_v, out_m,
    h_send, h_recv, w_buf, v_buf, m_buf, z_hi, z_lo, h_hi, h_lo, v_base,
    halo_s, halo_r, w_s, w_r, v_s, v_r, m_s, m_r, own_s,
):
    sky, exp = lax.axis_index("sky"), lax.axis_index("exp")
    after, before = lax.rem(sky + 1, N_SKY), lax.rem(sky + N_SKY - 1, N_SKY)
    peers = [lax.rem(exp + d, N_EXP) for d in range(N_EXP)]

    m_buf[...] = jnp.zeros((8, LANES), I32)
    m_buf[0:1, 0:64] = dest[...] * PR + offs[...]
    low_half = iota((8, HALF), 0) < 4

    def pack(e, _):
        h_send[0, e, 0] = image[e, 16:24, 0:HALF]
        h_send[0, e, 1] = image[e, 24:32, 0:HALF]
        h_send[0, e, 2] = image[e, 16:24, HALF:COLS]
        h_send[0, e, 3] = image[e, 24:32, HALF:COLS]
        h_send[0, e, 4] = jnp.where(
            low_half, pltpu.roll(image[e, 8:16, HALF:COLS], 4, 0), image[e, 8:16, 0:HALF]
        )
        h_send[1, e, 0] = image[e, 0:8, 0:HALF]
        h_send[1, e, 1] = image[e, 8:16, 0:HALF]
        h_send[1, e, 2] = image[e, 0:8, HALF:COLS]
        h_send[1, e, 3] = image[e, 8:16, HALF:COLS]
        h_send[1, e, 4] = jnp.where(
            low_half, image[e, 16:24, 0:HALF], pltpu.roll(image[e, 16:24, HALF:COLS], 4, 0)
        )
        return 0

    lax.fori_loop(0, EXPS, pack, 0)

    greet([(after, exp), (before, exp)] + [(sky, q) for q in peers[1:]])

    def halo(direction, e):
        return pltpu.make_async_remote_copy(
            src_ref=h_send.at[direction, e],
            dst_ref=h_recv.at[direction, e],
            send_sem=halo_s.at[direction, e],
            recv_sem=halo_r.at[direction, e],
            device_id=(after if direction == 0 else before, exp),
            device_id_type=MESH,
        )

    def start_halo(e, _):
        halo(0, e).start()
        halo(1, e).start()
        return 0

    lax.fori_loop(0, EXPS, start_halo, 0)

    def meta(d):
        return pltpu.make_async_remote_copy(
            src_ref=m_buf, dst_ref=out_m.at[exp], send_sem=m_s.at[d], recv_sem=m_r.at[d],
            device_id=(sky, peers[d]), device_id_type=MESH,
        )

    for d in range(1, N_EXP):
        meta(d).start()

    def weights(eb, _):
        e, rb = eb // 4, lax.rem(eb, 4)
        rows = pl.ds(pl.multiple_of(rb * 8, 8), 8)
        for part in range(2):
            for q in range(N_EXP):
                lane = part * HALF + q * LANES
                w_buf[q, eb, part] = 1.0 / variance[e, rows, lane:lane + LANES]
        return 0

    lax.fori_loop(0, BLOCKS, weights, 0)

    def send_w(d):
        return pltpu.make_async_remote_copy(
            src_ref=w_buf.at[peers[d]], dst_ref=out_w.at[exp], send_sem=w_s.at[d], recv_sem=w_r.at[d],
            device_id=(sky, peers[d]), device_id_type=MESH,
        )

    for d in range(1, N_EXP):
        send_w(d).start()

    own_w = pltpu.make_async_copy(w_buf.at[exp], out_w.at[exp], own_s.at[0])
    own_m = pltpu.make_async_copy(m_buf, out_m.at[exp], own_s.at[1])
    own_w.start()
    own_m.start()

    k3 = iota((ROWS, STEP), 1)
    k = lax.rem(k3, 80)
    source = jnp.where(
        k < 32, k, jnp.where(k < 48, k - 48, jnp.where(k < 68, k - 16, jnp.where(k < 72, k - 88, 1000)))
    )
    source = jnp.where(k3 < 240, source, 1000)
    source = jnp.where((source < 0) & (sky == 0), 1000, source)
    source = jnp.where((source >= ROWS) & (sky == N_SKY - 1), 1000, source)
    row_lag = source - iota((ROWS, STEP), 0) + RIM

    def row_band(b, _):
        def tap(t, band):
            return jnp.where(row_lag == t, row_taps[b, t], band)

        v_base[b] = lax.fori_loop(0, TAPS, tap, jnp.zeros((ROWS, STEP), F32))
        return 0

    lax.fori_loop(0, NB, row_band, 0)

    h_hi[...] = jnp.zeros(h_hi.shape, BF16)
    h_lo[...] = jnp.zeros(h_lo.shape, BF16)
    col_diff = iota((LANES, LANES), 0) - iota((LANES, LANES), 1) + RIM

    def col_band(b, _):
        for shift in (-1, 0, 1):
            lag = col_diff + LANES * shift

            def tap(t, band):
                return jnp.where(lag == t, col_taps[b, t], band)

            high, low = split(lax.fori_loop(0, TAPS, tap, jnp.zeros((LANES, LANES), F32)))
            for u in range(2):
                rows = slice((u + 1 + shift) * LANES, (u + 2 + shift) * LANES)
                h_hi[b, rows, u * LANES:(u + 1) * LANES] = high
                h_lo[b, rows, u * LANES:(u + 1) * LANES] = low
        return 0

    lax.fori_loop(0, NB, col_band, 0)

    for z in (z_hi, z_lo):
        z[:, :, 0:LANES] = jnp.zeros((NB, PER * ROWS, LANES), BF16)
        z[:, :, LANES + COLS:] = jnp.zeros((NB, PER * ROWS, LANES), BF16)

    third = lax.broadcasted_iota(I32, (NB * ROWS, STEP), 1) >= 160
    low_rows = iota((8, STEP), 0) < 4

    def send_v(c, d):
        span = pl.ds(c * (4 * PER), 4 * PER)
        return pltpu.make_async_remote_copy(
            src_ref=v_buf.at[peers[d], span], dst_ref=out_v.at[exp, span],
            send_sem=v_s.at[c, d], recv_sem=v_r.at[c, d],
            device_id=(sky, peers[d]), device_id_type=MESH,
        )

    def chunk(c, _):
        def vertical(el, _):
            e = c * PER + el
            halo(0, e).wait_recv()
            halo(1, e).wait_recv()
            table_row = coef_index[e]
            bands = [coef_table[table_row, b] * v_base[b] for b in range(NB)]
            high, low = split(jnp.concatenate(bands, 0))
            left = jnp.where(third, low.astype(F32), high.astype(F32)).astype(BF16)
            out_rows = pl.ds(pl.multiple_of(el * ROWS, ROWS), ROWS)
            for j in range(NSTEP):
                part, at = divmod(j * STEP, HALF)
                cols = slice(at, at + STEP)
                up = h_recv[0, e, 2 * part:2 * part + 2, :, cols].reshape(16, STEP)
                down = h_recv[1, e, 2 * part:2 * part + 2, :, cols].reshape(16, STEP)
                up4, down4 = h_recv[0, e, 4, :, cols], h_recv[1, e, 4, :, cols]
                if part == 0:
                    rest = jnp.where(low_rows, down4, up4)
                else:
                    rest = pltpu.roll(jnp.where(low_rows, up4, down4), 4, 0)
                x = jnp.concatenate(
                    [image[e, :, j * STEP:(j + 1) * STEP], up, down, rest, jnp.zeros((8, STEP), F32)], 0
                )
                x_hi, x_lo = split(x)
                right = jnp.concatenate([x_hi, x_lo, x_hi, jnp.zeros((16, STEP), BF16)], 0)
                z = jnp.dot(left, right, preferred_element_type=F32)
                high_z, low_z = split(z)
                at = LANES + j * STEP
                z_hi[:, out_rows, at:at + STEP] = high_z.reshape(NB, ROWS, STEP)
                z_lo[:, out_rows, at:at + STEP] = low_z.reshape(NB, ROWS, STEP)
            return 0

        lax.fori_loop(0, PER, vertical, 0)

        def horizontal(j, _):
            cols = pl.ds(pl.multiple_of(j * STEP, STEP), 2 * STEP)
            total = jnp.zeros((PER * ROWS, STEP), F32)
            for b in range(NB):
                zh, zl = z_hi[b, :, cols], z_lo[b, :, cols]
                total += jnp.dot(zh, h_hi[b], preferred_element_type=F32)
                total += jnp.dot(zl, h_hi[b], preferred_element_type=F32)
                total += jnp.dot(zh, h_lo[b], preferred_element_type=F32)
            part = j // 4
            span = pl.ds(c * (4 * PER), 4 * PER)
            for u in range(2):
                q = lax.rem(j, 4) * 2 + u
                piece = total[:, u * LANES:(u + 1) * LANES].reshape(4 * PER, 8, LANES)
                v_buf[q, span, part] = piece * w_buf[q, span, part]
            return 0

        lax.fori_loop(0, NSTEP, horizontal, 0)
        for d in range(1, N_EXP):
            send_v(c, d).start()
        return 0

    lax.fori_loop(0, CHUNKS, chunk, 0)

    own_v = pltpu.make_async_copy(v_buf.at[exp], out_v.at[exp], own_s.at[2])
    own_v.start()

    def end_halo(e, _):
        halo(0, e).wait_send()
        halo(1, e).wait_send()
        return 0

    lax.fori_loop(0, EXPS, end_halo, 0)
    for d in range(1, N_EXP):
        meta(d).wait()
        send_w(d).wait()
    own_w.wait()
    own_m.wait()
    own_v.wait()

    def end_v(c, _):
        for d in range(1, N_EXP):
            send_v(c, d).wait()
        return 0

    lax.fori_loop(0, CHUNKS, end_v, 0)


def match(image, variance, dest, offs, coef_index, coef_table, row_taps, col_taps):
    slabs = jax.ShapeDtypeStruct((N_EXP, BLOCKS, 2, 8, LANES), F32)
    vmem, smem, anywhere = (pl.BlockSpec(memory_space=s) for s in (pltpu.VMEM, pltpu.SMEM, pl.ANY))
    dma = pltpu.SemaphoreType.DMA
    return pl.pallas_call(
        match_kernel,
        out_shape=(slabs, slabs, jax.ShapeDtypeStruct((N_EXP, 8, LANES), I32)),
        in_specs=[vmem] * 4 + [smem] * 4,
        out_specs=(anywhere,) * 3,
        scratch_shapes=[
            pltpu.VMEM((2, EXPS, 5, 8, HALF), F32),
            pltpu.VMEM((2, EXPS, 5, 8, HALF), F32),
            pltpu.VMEM((N_EXP, BLOCKS, 2, 8, LANES), F32),
            pltpu.VMEM((N_EXP, BLOCKS, 2, 8, LANES), F32),
            pltpu.VMEM((8, LANES), I32),
            pltpu.VMEM((NB, PER * ROWS, COLS + 2 * LANES), BF16),
            pltpu.VMEM((NB, PER * ROWS, COLS + 2 * LANES), BF16),
            pltpu.VMEM((NB, 2 * STEP, STEP), BF16),
            pltpu.VMEM((NB, 2 * STEP, STEP), BF16),
            pltpu.VMEM((NB, ROWS, STEP), F32),
            dma((2, EXPS)), dma((2, EXPS)),
            dma((N_EXP,)), dma((N_EXP,)),
            dma((CHUNKS, N_EXP)), dma((CHUNKS, N_EXP)),
            dma((N_EXP,)), dma((N_EXP,)),
            dma((3,)),
        ],
        compiler_params=pltpu.CompilerParams(
            collective_id=0, has_side_effects=True, vmem_limit_bytes=50 * 1024 * 1024
        ),
    )(image, variance, dest, offs, coef_index, coef_table, row_taps, col_taps)


def place_kernel(rows, w, v, acc_w, acc_v):
    acc_w[...] = jnp.zeros((PATCH_ROWS, LANES), F32)
    acc_v[...] = jnp.zeros((PATCH_ROWS, LANES), F32)

    def group(source, _):
        def block(eb, _):
            for part in range(2):
                at = pl.ds(rows[source, 0, eb * 2 + part], 8)
                acc_w[at, :] += w[source, eb, part]
                acc_v[at, :] += v[source, eb, part]
            return 0

        return lax.fori_loop(0, BLOCKS, block, 0, unroll=4)

    lax.fori_loop(0, N_EXP, group, 0)


def place(rows, w, v):
    vmem, smem = (pl.BlockSpec(memory_space=s) for s in (pltpu.VMEM, pltpu.SMEM))
    dense = jax.ShapeDtypeStruct((PATCH_ROWS, LANES), F32)
    return pl.pallas_call(
        place_kernel,
        out_shape=(dense, dense),
        in_specs=[smem, vmem, vmem],
        out_specs=(vmem, vmem),
        compiler_params=pltpu.CompilerParams(vmem_limit_bytes=40 * 1024 * 1024),
    )(rows, w, v)


class Ring:
    def __init__(self, size, me, target, chunk, half, land, send, recv):
        self.size, self.me, self.target = size, me, target
        self.chunk, self.half, self.land = chunk, half, land
        self.send, self.recv = send, recv
        self.steps = size // 2

    def owner(self, way, distance):
        return lax.rem(self.me + (distance if way == 0 else self.size - distance), self.size)

    def copy(self, src, dst, way, number):
        return pltpu.make_async_remote_copy(
            src_ref=src, dst_ref=dst, send_sem=self.send.at[way, number], recv_sem=self.recv.at[way, number],
            device_id=self.target(self.owner(way, 1)), device_id_type=MESH,
        )

    def copies(self, way, step):
        own = self.chunk(self.owner(way, self.steps - step))
        here = self.land.at[way, step]
        if step == 0:
            return [self.copy(self.half(own, way), self.half(here, way), way, 0)], []
        came = self.land.at[way, step - 1]
        if step == 1:
            early = [self.copy(self.half(own, 1 - way), self.half(here, 1 - way), way, 1)]
            return early, [self.copy(self.half(came, way), self.half(here, way), way, 2)]
        return [], [self.copy(came, here, way, step + 1)]

    def begin(self):
        for step in (0, 1):
            for way in (0, 1):
                for copy in self.copies(way, step)[0]:
                    copy.start()

    def arrived(self, way, step):
        early, late = self.copies(way, step)
        for copy in early + late:
            copy.wait_recv()

    def advance(self, step):
        for way in (0, 1):
            self.arrived(way, step - 1)
            came = self.land.at[way, step - 1]
            own = self.chunk(self.owner(way, self.steps - step))
            if step == 1:
                came, own = self.half(came, way), self.half(own, way)
            came[...] = came[...] + own[...]
            for copy in self.copies(way, step)[1]:
                copy.start()

    def total(self):
        last = self.steps - 1
        for way in (0, 1):
            self.arrived(way, last)
        return self.chunk(self.me)[...] + self.land[0, last] + self.land[1, last]

    def drain(self):
        for step in range(self.steps):
            for way in (0, 1):
                early, late = self.copies(way, step)
                for copy in early + late:
                    copy.wait_send()


def gather_kernel(
    acc_w, acc_v, out_c, out_w,
    land1, land2, land3, land4, mid_v, mid_w, last, rows,
    s1, r1, s2, r2, s3, r3, s4, r4, row_s, row_r,
):
    sky, exp = lax.axis_index("sky"), lax.axis_index("exp")
    z, x = sky // NX, lax.rem(sky, NX)
    peers = [lax.rem(exp + d, N_EXP) for d in range(N_EXP)]

    def at_x(other):
        return (z * NX + other, exp)

    def at_z(other):
        return (other * NX + x, exp)

    greet(
        [at_x(lax.rem(x + 1, NX)), at_x(lax.rem(x + NX - 1, NX)),
         at_z(lax.rem(z + 1, NZ)), at_z(lax.rem(z + NZ - 1, NZ))]
        + [(sky, q) for q in peers[1:]]
    )

    def halves(size):
        def half(ref, which):
            return ref.at[which * size:(which + 1) * size]

        return half

    v_x = Ring(NX, x, at_x, lambda o: acc_v.at[:, o], halves(NZ // 2), land1, s1, r1)
    w_z = Ring(NZ, z, at_z, lambda o: acc_w.at[o], halves(NX // 2), land2, s2, r2)
    v_z = Ring(NZ, z, at_z, lambda o: mid_v.at[o], halves(PR // 2), land3, s3, r3)
    w_x = Ring(NX, x, at_x, lambda o: mid_w.at[o], halves(PR // 2), land4, s4, r4)

    w_z.begin()
    v_x.begin()
    w_z.advance(1)
    v_x.advance(1)
    w_z.advance(2)
    mid_v[...] = v_x.total()
    w_z.advance(3)
    v_z.begin()
    v_z.advance(1)
    mid_w[...] = w_z.total()
    w_x.begin()
    v_z.advance(2)
    w_x.advance(1)
    v_z.advance(3)
    weight = w_x.total()
    last[1] = weight
    last[0] = v_z.total() / (1.0 + weight)

    def rows_copy(d):
        return pltpu.make_async_remote_copy(
            src_ref=last.at[:, pl.ds(pl.multiple_of(peers[d] * 16, 16), 16)],
            dst_ref=rows.at[exp],
            send_sem=row_s.at[d], recv_sem=row_r.at[d],
            device_id=(sky, peers[d]), device_id_type=MESH,
        )

    for d in range(1, N_EXP):
        rows_copy(d).start()
    rows[exp] = last[:, pl.ds(pl.multiple_of(exp * 16, 16), 16)]
    for d in range(1, N_EXP):
        rows_copy(d).wait_recv()
    for q in range(N_EXP):
        out_c[:, q * LANES:(q + 1) * LANES] = rows[q, 0]
        out_w[:, q * LANES:(q + 1) * LANES] = rows[q, 1]
    for d in range(1, N_EXP):
        rows_copy(d).wait_send()
    for ring in (v_x, w_z, v_z, w_x):
        ring.drain()


def gather(acc_w, acc_v):
    vmem = pl.BlockSpec(memory_space=pltpu.VMEM)
    out = jax.ShapeDtypeStruct((PR // N_EXP, HALF), F32)
    dma = pltpu.SemaphoreType.DMA
    return pl.pallas_call(
        gather_kernel,
        out_shape=(out, out),
        in_specs=[vmem, vmem],
        out_specs=(vmem, vmem),
        scratch_shapes=[
            pltpu.VMEM((2, 2, NZ, PR, LANES), F32),
            pltpu.VMEM((2, 4, NX, PR, LANES), F32),
            pltpu.VMEM((2, 4, PR, LANES), F32),
            pltpu.VMEM((2, 2, PR, LANES), F32),
            pltpu.VMEM((NZ, PR, LANES), F32),
            pltpu.VMEM((NX, PR, LANES), F32),
            pltpu.VMEM((2, PR, LANES), F32),
            pltpu.VMEM((N_EXP, 2, PR // N_EXP, LANES), F32),
            dma((2, 3)), dma((2, 3)), dma((2, 5)), dma((2, 5)),
            dma((2, 5)), dma((2, 5)), dma((2, 3)), dma((2, 3)),
            dma((N_EXP,)), dma((N_EXP,)),
        ],
        compiler_params=pltpu.CompilerParams(
            collective_id=1, has_side_effects=True, vmem_limit_bytes=40 * 1024 * 1024
        ),
    )(acc_w.reshape(NZ, NX, PR, LANES), acc_v.reshape(NZ, NX, PR, LANES))


def per_device(image, variance, coef_index, coef_table, row_taps, col_taps, destination, offset):
    slab_w, slab_v, rows = match(
        image, variance, destination.reshape(1, -1), offset.reshape(1, -1),
        coef_index, coef_table, row_taps, col_taps,
    )
    acc_w, acc_v = place(rows, slab_w, slab_v)
    return gather(acc_w, acc_v)


def solution(mesh):
    placed = (
        P("exp", "sky", None),
        P("exp", "sky", None),
        P("exp"),
        P(),
        P(),
        P(),
        P("exp", "sky", None, None),
        P("exp", "sky", None),
    )
    return jax.shard_map(
        per_device,
        mesh=mesh,
        in_specs=placed,
        out_specs=(P(("sky", "exp"), None), P(("sky", "exp"), None)),
        check_vma=False,
    )
```

time: 487 us -> 120 us (0.25)
  the two profiles are of different devices: /device:TPU:4 before, /device:TPU:1 now
where the time goes in v1:
time: 120 us; the launch traced here: 119 us
  Pallas kernels  112 us (93%)
  local copies, waits for them, and re-layouts  6.95 us (6%)
    pallas_call x1, Pallas kernels, match(): pl.pallas_call(match_kernel, out_shape=(slabs, slabs, jax.ShapeDtypeStruc...  63.6 us
    pallas_call x1, Pallas kernels, gather(): pl.pallas_call(gather_kernel, out_shape=(out, out), in_specs=[vmem, vmem]...  44.3 us
    unnamed x15, local copies, waits for them, and re-layouts  6.95 us
    pallas_call x1, Pallas kernels, place(): pl.pallas_call(place_kernel, out_shape=(dense, dense), in_specs=[smem, vm...  3.9 us

profile of v1, /device:TPU:1, one launch (start us, length us, event | category | flops | bytes accessed | tf_op | source)
XLA Modules:
  0.0 119.3 jit_solution(14208292559048428435)
XLA Ops:
  0.6 0.8 copy.10.coef_table
  1.4 0.0 copy-start.1
  1.4 0.7 copy-done.1
  2.1 0.0 copy-start.2
  2.1 0.7 copy-done.2
  2.8 0.0 copy-start.3
  2.8 0.7 copy-done.3
  3.4 0.0 copy-start.4
  3.4 0.7 copy-done.4
  4.1 0.0 copy-start.5
  4.1 0.7 copy-done.5
  4.7 63.6 %shard_map.95 = (f32[8,32,2,8,128]{4,3,2,1,0:T(8,128)S(1)}, f32[8,32,2,8,128]{4,3,2,1,0:T(8,128)}, s32[8,8,128]{2,1,0:T(8,128)S(1)}) custom-call(f32[8,32,2048]{2,1,0:T(8,128)} %image.1, f32[8,32,2048]{2,1,0:T(8,128)} %variance.1, s32[1,64]{1,0:T(1,128)S(1)} %bitcast.6, s32[1,64]{1,0:T(1,128)S(1)} %bitcast.7, s32[8]{0:T(128)S(1)} %copy-done.5, ...), custom_call_target="tpu_custom_call" | custom-call | tf_op jit(solution)/shard_map/pallas_call | solution.py:264
  68.3 0.0 copy-start
  68.3 1.6 %copy-done = f32[8,32,2,8,128]{4,3,2,1,0:T(8,128)S(1)} copy-done((f32[8,32,2,8,128]{4,3,2,1,0:T(8,128)S(1)}, f32[8,32,2,8,128]{4,3,2,1,0:T(8,128)}, u32[]{:S(2)}) %copy-start) | copy-done | bytes 2097176
  69.9 3.9 %shard_map.96 = (f32[4096,128]{1,0:T(8,128)S(1)}, f32[4096,128]{1,0:T(8,128)S(1)}) custom-call(s32[8,8,128]{2,1,0:T(8,128)S(1)} %get-tuple-element.7.rows, f32[8,32,2,8,128]{4,3,2,1,0:T(8,128)S(1)} %get-tuple-element.8.w, f32[8,32,2,8,128]{4,3,2,1,0:T(8,128)S(1)} %copy-done), custom_call_target="tpu_custom_call" | custom-call | tf_op jit(solution)/shard_map/pallas_call | solution.py:312
  73.8 44.3 %shard_map.97 = (f32[16,1024]{1,0:T(8,128)S(1)}, f32[16,1024]{1,0:T(8,128)S(1)}) custom-call(f32[8,4,128,128]{3,2,1,0:T(8,128)S(1)} %bitcast.4, f32[8,4,128,128]{3,2,1,0:T(8,128)S(1)} %bitcast.5), custom_call_target="tpu_custom_call" | custom-call | tf_op jit(solution)/shard_map/pallas_call | solution.py:460
  118.1 0.6 copy.13
  118.7 0.6 copy.14
Async XLA Ops:
  1.4 0.7 copy-start.1
  2.1 0.7 copy-start.2
  2.8 0.7 copy-start.3
  3.4 0.7 copy-start.4
  4.1 0.7 copy-start.5
  68.3 1.6 %copy-start = (f32[8,32,2,8,128]{4,3,2,1,0:T(8,128)S(1)}, f32[8,32,2,8,128]{4,3,2,1,0:T(8,128)}, u32[]{:S(2)}) copy-start(f32[8,32,2,8,128]{4,3,2,1,0:T(8,128)} %get-tuple-element.9.v) | copy-start | bytes 6291460

commit v2 on v0

v2 whole, which is shorter than its diff:
```python
import jax
import jax.numpy as jnp
from jax import lax
from jax.experimental import pallas as pl
from jax.experimental.pallas import tpu as pltpu
from jax.sharding import PartitionSpec as P

MESH = pl.DeviceIdType.MESH
F32, BF16, I32 = jnp.float32, jnp.bfloat16, jnp.int32

NB, TAPS, RIM = 5, 41, 20
N_SKY, N_EXP, NX, NZ = 32, 8, 4, 8
EXPS, ROWS, COLS, HALF = 8, 32, 2048, 1024
BLOCKS = EXPS * ROWS // 8
LANES = 128
PR, PATCH_ROWS = 128, 4096
PER = 4
CHUNKS = EXPS // PER
STEP = 256
NSTEP = COLS // STEP


def iota(shape, dim):
    return lax.broadcasted_iota(I32, shape, dim)


def greet(devices):
    barrier = pltpu.get_barrier_semaphore()
    for device in devices:
        pl.semaphore_signal(barrier, inc=1, device_id=device, device_id_type=MESH)
    pl.semaphore_wait(barrier, len(devices))


def split(value):
    high = value.astype(BF16)
    return high, (value - high.astype(F32)).astype(BF16)

SLOTS = 4
EMPTY = -4096


def strip_table(dest, offs):
    sub, lane = iota((64, LANES), 0), iota((64, LANES), 1)
    line = jnp.concatenate([dest, jnp.full((1, 64), -1, I32)], 1)
    shift = jnp.concatenate([offs, jnp.zeros((1, 64), I32)], 1)
    diagonal = sub == lane
    patch = jnp.sum(jnp.where(diagonal, line, 0), 1, keepdims=True)
    first = jnp.sum(jnp.where(diagonal, shift, 0), 1, keepdims=True)
    rank = jnp.sum(jnp.where((patch == line) & (lane < sub), 1, 0), 1, keepdims=True)
    here = patch * SLOTS + rank == lane
    strip = jnp.sum(jnp.where(here, sub, 0), 0, keepdims=True)
    start = jnp.sum(jnp.where(here, first - EMPTY, 0), 0, keepdims=True) + EMPTY
    row = iota((8, LANES), 0)
    return jnp.where(row == 0, strip, jnp.where(row == 1, start, 0))


class Ring:
    def __init__(self, size, me, target, chunk, half, land, send, recv):
        self.size, self.me, self.target = size, me, target
        self.chunk, self.half, self.land = chunk, half, land
        self.send, self.recv = send, recv
        self.steps = size // 2

    def owner(self, way, distance):
        return lax.rem(self.me + (distance if way == 0 else self.size - distance), self.size)

    def copy(self, src, dst, way, number):
        return pltpu.make_async_remote_copy(
            src_ref=src, dst_ref=dst, send_sem=self.send.at[way, number], recv_sem=self.recv.at[way, number],
            device_id=self.target(self.owner(way, 1)), device_id_type=MESH,
        )

    def copies(self, way, step):
        own = self.chunk(self.owner(way, self.steps - step))
        here = self.land.at[way, step]
        if step == 0:
            return [self.copy(self.half(own, way), self.half(here, way), way, 0)], []
        came = self.land.at[way, step - 1]
        if step == 1:
            early = [self.copy(self.half(own, 1 - way), self.half(here, 1 - way), way, 1)]
            return early, [self.copy(self.half(came, way), self.half(here, way), way, 2)]
        return [], [self.copy(came, here, way, step + 1)]

    def begin(self):
        for step in (0, 1):
            for way in (0, 1):
                for copy in self.copies(way, step)[0]:
                    copy.start()

    def arrived(self, way, step):
        early, late = self.copies(way, step)
        for copy in early + late:
            copy.wait_recv()

    def advance(self, step):
        for way in (0, 1):
            self.arrived(way, step - 1)
            came = self.land.at[way, step - 1]
            own = self.chunk(self.owner(way, self.steps - step))
            if step == 1:
                came, own = self.half(came, way), self.half(own, way)
            came[...] = came[...] + own[...]
            for copy in self.copies(way, step)[1]:
                copy.start()

    def total(self):
        last = self.steps - 1
        for way in (0, 1):
            self.arrived(way, last)
        return self.chunk(self.me)[...] + self.land[0, last] + self.land[1, last]

    def drain(self):
        for step in range(self.steps):
            for way in (0, 1):
                early, late = self.copies(way, step)
                for copy in early + late:
                    copy.wait_send()


def coadd_kernel(
    image_in, variance_in, dest, offs, coef_index, coef_table, row_taps, col_taps,
    out,
    image, variance, h_send, h_recv, w_buf, v_buf, w_got, v_got, m_buf, m_got, m_smem, slots,
    z_hi, z_lo, h_hi, h_lo, v_base, acc_w, acc_v,
    land_wz, land_wx, land_ax, land_az, land_bz, land_bx, mid_w, mid_a, mid_b, fin_w, fin_v, rows_w, rows_v,
    load_s, halo_s, halo_r, w_s, w_r, v_s, v_r, m_s, m_r, own_s,
    wz_s, wz_r, wx_s, wx_r, ax_s, ax_r, az_s, az_r, bz_s, bz_r, bx_s, bx_r, rw_s, rw_r, rv_s, rv_r,
):
    sky, exp = lax.axis_index("sky"), lax.axis_index("exp")
    z, x = sky // NX, lax.rem(sky, NX)
    after, before = lax.rem(sky + 1, N_SKY), lax.rem(sky + N_SKY - 1, N_SKY)
    peers = [lax.rem(exp + d, N_EXP) for d in range(N_EXP)]

    def at_x(other):
        return (z * NX + other, exp)

    def at_z(other):
        return (other * NX + x, exp)

    load_image = pltpu.make_async_copy(image_in, image, load_s.at[0])
    load_variance = pltpu.make_async_copy(variance_in, variance, load_s.at[1])
    load_image.start()
    load_variance.start()

    partners = [(after, exp), (before, exp)] + [(sky, q) for q in peers[1:]] + [
        at_x(lax.rem(x + 1, NX)), at_x(lax.rem(x + NX - 1, NX)),
        at_z(lax.rem(z + 1, NZ)), at_z(lax.rem(z + NZ - 1, NZ)),
    ]
    barrier = pltpu.get_barrier_semaphore()
    for device in partners:
        pl.semaphore_signal(barrier, inc=1, device_id=device, device_id_type=MESH)

    m_buf[...] = strip_table(dest[...], offs[...])
    load_image.wait()
    low_half = iota((8, HALF), 0) < 4

    def pack(e, _):
        h_send[0, e, 0] = image[e, 16:24, 0:HALF]
        h_send[0, e, 1] = image[e, 24:32, 0:HALF]
        h_send[0, e, 2] = image[e, 16:24, HALF:COLS]
        h_send[0, e, 3] = image[e, 24:32, HALF:COLS]
        h_send[0, e, 4] = jnp.where(
            low_half, pltpu.roll(image[e, 8:16, HALF:COLS], 4, 0), image[e, 8:16, 0:HALF]
        )
        h_send[1, e, 0] = image[e, 0:8, 0:HALF]
        h_send[1, e, 1] = image[e, 8:16, 0:HALF]
        h_send[1, e, 2] = image[e, 0:8, HALF:COLS]
        h_send[1, e, 3] = image[e, 8:16, HALF:COLS]
        h_send[1, e, 4] = jnp.where(
            low_half, image[e, 16:24, 0:HALF], pltpu.roll(image[e, 16:24, HALF:COLS], 4, 0)
        )
        return 0

    lax.fori_loop(0, EXPS, pack, 0)
    pl.semaphore_wait(barrier, len(partners))

    def halo(direction, e):
        return pltpu.make_async_remote_copy(
            src_ref=h_send.at[direction, e],
            dst_ref=h_recv.at[direction, e],
            send_sem=halo_s.at[direction, e],
            recv_sem=halo_r.at[direction, e],
            device_id=(after if direction == 0 else before, exp),
            device_id_type=MESH,
        )

    def start_halo(e, _):
        halo(0, e).start()
        halo(1, e).start()
        return 0

    lax.fori_loop(0, EXPS, start_halo, 0)

    def meta(d):
        return pltpu.make_async_remote_copy(
            src_ref=m_buf, dst_ref=m_got.at[exp], send_sem=m_s.at[d], recv_sem=m_r.at[d],
            device_id=(sky, peers[d]), device_id_type=MESH,
        )

    for d in range(1, N_EXP):
        meta(d).start()
    m_got[exp] = m_buf[...]

    load_variance.wait()

    def weights(eb, _):
        e, rb = eb // 4, lax.rem(eb, 4)
        rows = pl.ds(pl.multiple_of(rb * 8, 8), 8)
        for part in range(2):
            for q in range(N_EXP):
                lane = part * HALF + q * LANES
                w_buf[q, eb * 2 + part] = 1.0 / variance[e, rows, lane:lane + LANES]
        return 0

    lax.fori_loop(0, BLOCKS, weights, 0)

    def send_w(d):
        return pltpu.make_async_remote_copy(
            src_ref=w_buf.at[peers[d]], dst_ref=w_got.at[exp], send_sem=w_s.at[d], recv_sem=w_r.at[d],
            device_id=(sky, peers[d]), device_id_type=MESH,
        )

    for d in range(1, N_EXP):
        send_w(d).start()
    own_w = pltpu.make_async_copy(w_buf.at[exp], w_got.at[exp], own_s.at[0])
    own_w.start()

    k3 = iota((ROWS, STEP), 1)
    k = lax.rem(k3, 80)
    source = jnp.where(
        k < 32, k, jnp.where(k < 48, k - 48, jnp.where(k < 68, k - 16, jnp.where(k < 72, k - 88, 1000)))
    )
    source = jnp.where(k3 < 240, source, 1000)
    source = jnp.where((source < 0) & (sky == 0), 1000, source)
    source = jnp.where((source >= ROWS) & (sky == N_SKY - 1), 1000, source)
    row_lag = source - iota((ROWS, STEP), 0) + RIM

    def row_band(b, _):
        def tap(t, band):
            return jnp.where(row_lag == t, row_taps[b, t], band)

        v_base[b] = lax.fori_loop(0, TAPS, tap, jnp.zeros((ROWS, STEP), F32))
        return 0

    lax.fori_loop(0, NB, row_band, 0)

    h_hi[...] = jnp.zeros(h_hi.shape, BF16)
    h_lo[...] = jnp.zeros(h_lo.shape, BF16)
    col_diff = iota((LANES, LANES), 0) - iota((LANES, LANES), 1) + RIM

    def col_band(b, _):
        for shift in (-1, 0, 1):
            lag = col_diff + LANES * shift

            def tap(t, band):
                return jnp.where(lag == t, col_taps[b, t], band)

            high, low = split(lax.fori_loop(0, TAPS, tap, jnp.zeros((LANES, LANES), F32)))
            for u in range(2):
                rows = slice((u + 1 + shift) * LANES, (u + 2 + shift) * LANES)
                h_hi[b, rows, u * LANES:(u + 1) * LANES] = high
                h_lo[b, rows, u * LANES:(u + 1) * LANES] = low
        return 0

    lax.fori_loop(0, NB, col_band, 0)

    for part_z in (z_hi, z_lo):
        part_z[:, :, 0:LANES] = jnp.zeros((NB, PER * ROWS, LANES), BF16)
        part_z[:, :, LANES + COLS:] = jnp.zeros((NB, PER * ROWS, LANES), BF16)

    for d in range(1, N_EXP):
        meta(d).wait_recv()
    table = pltpu.make_async_copy(m_got, m_smem, own_s.at[1])
    table.start()
    table.wait()

    lane = iota((8, 2 * LANES), 1)
    lane_slot, lane_row = lane >> 3, lane & 7
    patch_row = iota((PR, 2 * LANES), 0)

    def select_rows(p, _):
        target = jnp.zeros((8, 2 * LANES), I32)
        for g in range(N_EXP):
            for j in range(SLOTS):
                target = jnp.where(lane_slot == g * SLOTS + j, m_smem[g, 1, p * SLOTS + j], target)
        target = (target + lane_row)[0:1]
        slots[p] = jnp.where(patch_row == target, 1.0, 0.0).astype(BF16)
        return 0

    lax.fori_loop(0, N_SKY, select_rows, 0)

    def add_strips(got, acc, p):
        tiles = [
            got[g, m_smem[g, 0, p * SLOTS + j] & (2 * BLOCKS - 1)] for g in range(N_EXP) for j in range(SLOTS)
        ]
        high, low = split(jnp.concatenate(tiles, 0))
        both = jnp.dot(slots[p], jnp.concatenate([high, low], 1), preferred_element_type=F32)
        acc[p // NX, lax.rem(p, NX)] = both[:, 0:LANES] + both[:, LANES:]

    def halves(size):
        def half(ref, which):
            return ref.at[which * size:(which + 1) * size]

        return half

    top, low_part = pl.ds(0, PR // 2), pl.ds(PR // 2, PR // 2)
    w_z = Ring(NZ, z, at_z, lambda o: acc_w.at[o], halves(NX // 2), land_wz, wz_s, wz_r)
    w_x = Ring(NX, x, at_x, lambda o: mid_w.at[o], halves(PR // 2), land_wx, wx_s, wx_r)
    a_x = Ring(NX, x, at_x, lambda o: acc_v.at[:, o, top], halves(NZ // 2), land_ax, ax_s, ax_r)
    a_z = Ring(NZ, z, at_z, lambda o: mid_a.at[o], halves(PR // 4), land_az, az_s, az_r)
    b_z = Ring(NZ, z, at_z, lambda o: acc_v.at[o, :, low_part], halves(NX // 2), land_bz, bz_s, bz_r)
    b_x = Ring(NX, x, at_x, lambda o: mid_b.at[o], halves(PR // 4), land_bx, bx_s, bx_r)

    def send_v(c, d):
        span = pl.ds(c * (8 * PER), 8 * PER)
        return pltpu.make_async_remote_copy(
            src_ref=v_buf.at[peers[d], span], dst_ref=v_got.at[exp, span],
            send_sem=v_s.at[c, d], recv_sem=v_r.at[c, d],
            device_id=(sky, peers[d]), device_id_type=MESH,
        )

    third = iota((NB * ROWS, STEP), 1) >= 160
    low_rows = iota((8, STEP), 0) < 4

    def chunk(c, _):
        @pl.when(c == CHUNKS - 1)
        def _():
            for d in range(1, N_EXP):
                send_w(d).wait_recv()
            own_w.wait()

            def add_weights(p, _):
                add_strips(w_got, acc_w, p)
                return 0

            lax.fori_loop(0, N_SKY, add_weights, 0)
            w_z.begin()

        def vertical(el, _):
            e = c * PER + el
            halo(0, e).wait_recv()
            halo(1, e).wait_recv()
            table_row = coef_index[e]
            bands = [coef_table[b, table_row] * v_base[b] for b in range(NB)]
            high, low = split(jnp.concatenate(bands, 0))
            left = jnp.where(third, low.astype(F32), high.astype(F32)).astype(BF16)
            out_rows = pl.ds(pl.multiple_of(el * ROWS, ROWS), ROWS)
            for j in range(NSTEP):
                part, at = divmod(j * STEP, HALF)
                cols = slice(at, at + STEP)
                up = h_recv[0, e, 2 * part:2 * part + 2, :, cols].reshape(16, STEP)
                down = h_recv[1, e, 2 * part:2 * part + 2, :, cols].reshape(16, STEP)
                up4, down4 = h_recv[0, e, 4, :, cols], h_recv[1, e, 4, :, cols]
                if part == 0:
                    rest = jnp.where(low_rows, down4, up4)
                else:
                    rest = pltpu.roll(jnp.where(low_rows, up4, down4), 4, 0)
                rows = jnp.concatenate(
                    [image[e, :, j * STEP:(j + 1) * STEP], up, down, rest, jnp.zeros((8, STEP), F32)], 0
                )
                x_hi, x_lo = split(rows)
                right = jnp.concatenate([x_hi, x_lo, x_hi, jnp.zeros((16, STEP), BF16)], 0)
                high_z, low_z = split(jnp.dot(left, right, preferred_element_type=F32))
                at = LANES + j * STEP
                z_hi[:, out_rows, at:at + STEP] = high_z.reshape(NB, ROWS, STEP)
                z_lo[:, out_rows, at:at + STEP] = low_z.reshape(NB, ROWS, STEP)
            return 0

        lax.fori_loop(0, PER, vertical, 0)

        def horizontal(j, _):
            cols = pl.ds(pl.multiple_of(j * STEP, STEP), 2 * STEP)
            total = jnp.zeros((PER * ROWS, STEP), F32)
            for b in range(NB):
                zh, zl = z_hi[b, :, cols], z_lo[b, :, cols]
                total += jnp.dot(zh, h_hi[b], preferred_element_type=F32)
                total += jnp.dot(zl, h_hi[b], preferred_element_type=F32)
                total += jnp.dot(zh, h_lo[b], preferred_element_type=F32)
            part = j // 4
            for u in range(2):
                q = lax.rem(j, 4) * 2 + u
                for r in range(4 * PER):
                    piece = total[r * 8:(r + 1) * 8, u * LANES:(u + 1) * LANES]
                    strip = (c * (4 * PER) + r) * 2 + part
                    v_buf[q, strip] = piece * w_buf[q, strip]
            return 0

        lax.fori_loop(0, NSTEP, horizontal, 0)
        for d in range(1, N_EXP):
            send_v(c, d).start()
        return 0

    lax.fori_loop(0, CHUNKS, chunk, 0)
    own_v = pltpu.make_async_copy(v_buf.at[exp], v_got.at[exp], own_s.at[2])
    own_v.start()

    w_z.advance(1)
    w_z.advance(2)
    w_z.advance(3)

    def arrived_v(c, _):
        for d in range(1, N_EXP):
            send_v(c, d).wait_recv()
        return 0

    lax.fori_loop(0, CHUNKS, arrived_v, 0)
    own_v.wait()

    def add_values(p, _):
        add_strips(v_got, acc_v, p)
        return 0

    lax.fori_loop(0, N_SKY, add_values, 0)
    a_x.begin()
    b_z.begin()
    mid_w[...] = w_z.total()
    w_x.begin()
    a_x.advance(1)
    b_z.advance(1)
    w_x.advance(1)
    b_z.advance(2)
    mid_a[...] = a_x.total()
    a_z.begin()
    b_z.advance(3)
    fin_w[...] = w_x.total()

    def rows_copy(fin, land, send, recv, d):
        return pltpu.make_async_remote_copy(
            src_ref=fin.at[pl.ds(pl.multiple_of(peers[d] * 16, 16), 16)],
            dst_ref=land.at[exp],
            send_sem=send.at[d], recv_sem=recv.at[d],
            device_id=(sky, peers[d]), device_id_type=MESH,
        )

    mine = pl.ds(pl.multiple_of(exp * 16, 16), 16)
    for d in range(1, N_EXP):
        rows_copy(fin_w, rows_w, rw_s, rw_r, d).start()
    rows_w[exp] = fin_w[mine]
    a_z.advance(1)
    mid_b[...] = b_z.total()
    b_x.begin()
    a_z.advance(2)
    b_x.advance(1)
    a_z.advance(3)
    fin_v[PR // 2:] = b_x.total()
    fin_v[:PR // 2] = a_z.total()
    for d in range(1, N_EXP):
        rows_copy(fin_v, rows_v, rv_s, rv_r, d).start()
    rows_v[exp] = fin_v[mine]
    for d in range(1, N_EXP):
        rows_copy(fin_w, rows_w, rw_s, rw_r, d).wait()
    for q in range(N_EXP):
        out[1, :, q * LANES:(q + 1) * LANES] = rows_w[q]

    def end_halo(e, _):
        halo(0, e).wait_send()
        halo(1, e).wait_send()
        return 0

    lax.fori_loop(0, EXPS, end_halo, 0)
    for d in range(1, N_EXP):
        meta(d).wait_send()
        send_w(d).wait_send()

    def end_v(c, _):
        for d in range(1, N_EXP):
            send_v(c, d).wait_send()
        return 0

    lax.fori_loop(0, CHUNKS, end_v, 0)
    for ring in (w_z, w_x, a_x, a_z, b_z, b_x):
        ring.drain()
    for d in range(1, N_EXP):
        rows_copy(fin_v, rows_v, rv_s, rv_r, d).wait()
    for q in range(N_EXP):
        out[0, :, q * LANES:(q + 1) * LANES] = rows_v[q]


def per_device(image, variance, coef_index, coef_table, row_taps, col_taps, destination, offset):
    vmem, smem, anywhere = (pl.BlockSpec(memory_space=s) for s in (pltpu.VMEM, pltpu.SMEM, pl.ANY))
    dma = pltpu.SemaphoreType.DMA

    def held(*shape, dtype=F32):
        return pltpu.VMEM(shape, dtype)

    strips = (N_EXP, 2 * BLOCKS, 8, LANES)
    sums = pl.pallas_call(
        coadd_kernel,
        out_shape=jax.ShapeDtypeStruct((2, PR // N_EXP, HALF), F32),
        in_specs=[anywhere] * 2 + [vmem] * 2 + [smem] * 4,
        out_specs=vmem,
        scratch_shapes=[
            held(EXPS, ROWS, COLS), held(EXPS, ROWS, COLS),
            held(2, EXPS, 5, 8, HALF), held(2, EXPS, 5, 8, HALF),
            held(*strips), held(*strips), held(*strips), held(*strips),
            held(8, LANES, dtype=I32), held(N_EXP, 8, LANES, dtype=I32),
            pltpu.SMEM((N_EXP, 8, LANES), I32),
            held(N_SKY, PR, 2 * LANES, dtype=BF16),
            held(NB, PER * ROWS, COLS + 2 * LANES, dtype=BF16),
            held(NB, PER * ROWS, COLS + 2 * LANES, dtype=BF16),
            held(NB, 2 * STEP, STEP, dtype=BF16),
            held(NB, 2 * STEP, STEP, dtype=BF16),
            held(NB, ROWS, STEP),
            held(NZ, NX, PR, LANES), held(NZ, NX, PR, LANES),
            held(2, 4, NX, PR, LANES), held(2, 2, PR, LANES),
            held(2, 2, NZ, PR // 2, LANES), held(2, 4, PR // 2, LANES),
            held(2, 4, NX, PR // 2, LANES), held(2, 2, PR // 2, LANES),
            held(NX, PR, LANES), held(NZ, PR // 2, LANES), held(NX, PR // 2, LANES),
            held(PR, LANES), held(PR, LANES),
            held(N_EXP, PR // N_EXP, LANES), held(N_EXP, PR // N_EXP, LANES),
            dma((2,)), dma((2, EXPS)), dma((2, EXPS)),
            dma((N_EXP,)), dma((N_EXP,)),
            dma((CHUNKS, N_EXP)), dma((CHUNKS, N_EXP)),
            dma((N_EXP,)), dma((N_EXP,)),
            dma((3,)),
        ] + [dma((2, n)) for n in (5, 5, 3, 3, 3, 3, 5, 5, 5, 5, 3, 3)] + [dma((N_EXP,))] * 4,
        compiler_params=pltpu.CompilerParams(
            collective_id=0, has_side_effects=True, vmem_limit_bytes=60 * 1024 * 1024
        ),
    )(
        image, variance, destination.reshape(1, -1), offset.reshape(1, -1),
        coef_index, coef_table.T, row_taps, col_taps,
    )
    return sums[0] / (1.0 + sums[1]), sums[1]


def solution(mesh):
    placed = (
        P("exp", "sky", None),
        P("exp", "sky", None),
        P("exp"),
        P(),
        P(),
        P(),
        P("exp", "sky", None, None),
        P("exp", "sky", None),
    )
    return jax.shard_map(
        per_device,
        mesh=mesh,
        in_specs=placed,
        out_specs=(P(("sky", "exp"), None), P(("sky", "exp"), None)),
        check_vma=False,
    )
```

time: 487 us -> 103 us (0.21)
  the two profiles are of different devices: /device:TPU:4 before, /device:TPU:1 now
where the time goes in v2:
time: 103 us
  Pallas kernels  101 us (98%)
  other arithmetic  1.53 us (1%)
    pallas_call x1, Pallas kernels, per_device(): pl.pallas_call(coadd_kernel, out_shape=jax.ShapeDtypeStruct((2, PR // N_E...  101 us

profile of v2, /device:TPU:1, one launch (start us, length us, event | category | flops | bytes accessed | tf_op | source)
XLA Modules:
  0.0 103.0 jit_solution(4853175317010157239)
XLA Ops:
  0.6 100.8 %shard_map.95 = f32[2,16,1024]{2,1,0:T(8,128)} custom-call(f32[8,32,2048]{2,1,0:T(8,128)} %image_in.1, f32[8,32,2048]{2,1,0:T(8,128)} %variance_in.1, s32[1,64]{1,0:T(1,128)} %bitcast.9, s32[1,64]{1,0:T(1,128)} %bitcast.10, s32[8]{0:T(128)} %coef_index.1, f32[5,16]{1,0:T(8,128)} %bitcast.8, f32[5,41]{1,0:T(8,128)} %row_taps.1, f32[5,41]{1,0:T(8,128)} %col_taps.1), custom_call_target="tpu_custom_call" | custom-call | tf_op jit(solution)/shard_map/pallas_call | solution.py:487
  101.4 1.5 %bitcast_divide_fusion = (f32[16,1024]{1,0:T(8,128)}, f32[16,1024]{1,0:T(8,128)}) fusion(f32[2,16,1024]{2,1,0:T(8,128)} %shard_map.95), kind=kLoop, calls=%fused_computation | loop fusion | flops 32768 | bytes 262144 | tf_op jit(solution)/shard_map/div | solution.py:524

commit v3 on v2

--- a/solution.py
+++ b/solution.py
@@ -14,8 +14,10 @@
 BLOCKS = EXPS * ROWS // 8
 LANES = 128
 PR, PATCH_ROWS = 128, 4096
-PER = 4
-CHUNKS = EXPS // PER
+SEND = 2
+CHUNKS = EXPS // SEND
+SLOTS_AT = 3
+WEIGHTS_AT = 6
 STEP = 256
 NSTEP = COLS // STEP
 
@@ -81,8 +83,8 @@
             return early, [self.copy(self.half(came, way), self.half(here, way), way, 2)]
         return [], [self.copy(came, here, way, step + 1)]
 
-    def begin(self):
-        for step in (0, 1):
+    def begin(self, *steps):
+        for step in steps or (0, 1):
             for way in (0, 1):
                 for copy in self.copies(way, step)[0]:
                     copy.start()
@@ -117,14 +119,42 @@
                     copy.wait_send()
 
 
+class Direct:
+    def __init__(self, size, me, target, chunk, land, send, recv):
+        self.size, self.me, self.target = size, me, target
+        self.chunk, self.land, self.send, self.recv = chunk, land, send, recv
+
+    def copy(self, d):
+        owner = lax.rem(self.me + d, self.size)
+        return pltpu.make_async_remote_copy(
+            src_ref=self.chunk(owner), dst_ref=self.land.at[d], send_sem=self.send.at[d], recv_sem=self.recv.at[d],
+            device_id=self.target(owner), device_id_type=MESH,
+        )
+
+    def begin(self):
+        for d in range(1, self.size):
+            self.copy(d).start()
+
+    def total(self):
+        total = self.chunk(self.me)[...]
+        for d in range(1, self.size):
+            self.copy(d).wait_recv()
+            total = total + self.land[d]
+        return total
+
+    def drain(self):
+        for d in range(1, self.size):
+            self.copy(d).wait_send()
+
+
 def coadd_kernel(
     image_in, variance_in, dest, offs, coef_index, coef_table, row_taps, col_taps,
     out,
     image, variance, h_send, h_recv, w_buf, v_buf, w_got, v_got, m_buf, m_got, m_smem, slots,
-    z_hi, z_lo, h_hi, h_lo, v_base, acc_w, acc_v,
-    land_wz, land_wx, land_ax, land_az, land_bz, land_bx, mid_w, mid_a, mid_b, fin_w, fin_v, rows_w, rows_v,
+    z_hi, z_lo, h_all, v_base, acc_w, acc_v,
+    land_ua, land_uaz, land_ub, land_ubx, land_a, land_az, land_b, land_bx, mid_ua, mid_ub, mid_a, mid_b, fin_w, fin_v, rows_w, rows_v,
     load_s, halo_s, halo_r, w_s, w_r, v_s, v_r, m_s, m_r, own_s,
-    wz_s, wz_r, wx_s, wx_r, ax_s, ax_r, az_s, az_r, bz_s, bz_r, bx_s, bx_r, rw_s, rw_r, rv_s, rv_r,
+    ua_s, ua_r, uaz_s, uaz_r, ub_s, ub_r, ubx_s, ubx_r, ax_s, ax_r, az_s, az_r, bz_s, bz_r, bx_s, bx_r, rw_s, rw_r, rv_s, rv_r,
 ):
     sky, exp = lax.axis_index("sky"), lax.axis_index("exp")
     z, x = sky // NX, lax.rem(sky, NX)
@@ -139,18 +169,28 @@
 
     load_image = pltpu.make_async_copy(image_in, image, load_s.at[0])
     load_variance = pltpu.make_async_copy(variance_in, variance, load_s.at[1])
+    load_variance.start()
     load_image.start()
-    load_variance.start()
 
     partners = [(after, exp), (before, exp)] + [(sky, q) for q in peers[1:]] + [
-        at_x(lax.rem(x + 1, NX)), at_x(lax.rem(x + NX - 1, NX)),
-        at_z(lax.rem(z + 1, NZ)), at_z(lax.rem(z + NZ - 1, NZ)),
-    ]
+        at_x(lax.rem(x + d, NX)) for d in range(1, NX)
+    ] + [at_z(lax.rem(z + d, NZ)) for d in range(1, NZ)]
     barrier = pltpu.get_barrier_semaphore()
     for device in partners:
         pl.semaphore_signal(barrier, inc=1, device_id=device, device_id_type=MESH)
 
-    m_buf[...] = strip_table(dest[...], offs[...])
+    load_variance.wait()
+
+    def weights(eb, _):
+        e, rb = eb // 4, lax.rem(eb, 4)
+        rows = pl.ds(pl.multiple_of(rb * 8, 8), 8)
+        for part in range(2):
+            for q in range(N_EXP):
+                lane = part * HALF + q * LANES
+                w_buf[q, eb * 2 + part] = 1.0 / variance[e, rows, lane:lane + LANES]
+        return 0
+
+    lax.fori_loop(0, BLOCKS, weights, 0)
     load_image.wait()
     low_half = iota((8, HALF), 0) < 4
 
@@ -172,6 +212,7 @@
         return 0
 
     lax.fori_loop(0, EXPS, pack, 0)
+    m_buf[...] = strip_table(dest[...], offs[...])
     pl.semaphore_wait(barrier, len(partners))
 
     def halo(direction, e):
@@ -184,44 +225,33 @@
             device_id_type=MESH,
         )
 
-    def start_halo(e, _):
-        halo(0, e).start()
-        halo(1, e).start()
-        return 0
-
-    lax.fori_loop(0, EXPS, start_halo, 0)
-
     def meta(d):
         return pltpu.make_async_remote_copy(
             src_ref=m_buf, dst_ref=m_got.at[exp], send_sem=m_s.at[d], recv_sem=m_r.at[d],
             device_id=(sky, peers[d]), device_id_type=MESH,
         )
 
+    def send_w(c, d):
+        span = pl.ds(c * (8 * SEND), 8 * SEND)
+        return pltpu.make_async_remote_copy(
+            src_ref=w_buf.at[peers[d], span], dst_ref=w_got.at[exp, span],
+            send_sem=w_s.at[c, d], recv_sem=w_r.at[c, d],
+            device_id=(sky, peers[d]), device_id_type=MESH,
+        )
+
     for d in range(1, N_EXP):
         meta(d).start()
     m_got[exp] = m_buf[...]
 
-    load_variance.wait()
-
-    def weights(eb, _):
-        e, rb = eb // 4, lax.rem(eb, 4)
-        rows = pl.ds(pl.multiple_of(rb * 8, 8), 8)
-        for part in range(2):
-            for q in range(N_EXP):
-                lane = part * HALF + q * LANES
-                w_buf[q, eb * 2 + part] = 1.0 / variance[e, rows, lane:lane + LANES]
-        return 0
-
-    lax.fori_loop(0, BLOCKS, weights, 0)
-
-    def send_w(d):
-        return pltpu.make_async_remote_copy(
-            src_ref=w_buf.at[peers[d]], dst_ref=w_got.at[exp], send_sem=w_s.at[d], recv_sem=w_r.at[d],
-            device_id=(sky, peers[d]), device_id_type=MESH,
-        )
-
-    for d in range(1, N_EXP):
-        send_w(d).start()
+    def start_sends(c, _):
+        for i in range(SEND):
+            halo(0, c * SEND + i).start()
+            halo(1, c * SEND + i).start()
+        for d in range(1, N_EXP):
+            send_w(c, d).start()
+        return 0
+
+    lax.fori_loop(0, CHUNKS, start_sends, 0)
     own_w = pltpu.make_async_copy(w_buf.at[exp], w_got.at[exp], own_s.at[0])
     own_w.start()
 
@@ -244,8 +274,7 @@
 
     lax.fori_loop(0, NB, row_band, 0)
 
-    h_hi[...] = jnp.zeros(h_hi.shape, BF16)
-    h_lo[...] = jnp.zeros(h_lo.shape, BF16)
+    h_all[...] = jnp.zeros(h_all.shape, BF16)
     col_diff = iota((LANES, LANES), 0) - iota((LANES, LANES), 1) + RIM
 
     def col_band(b, _):
@@ -257,22 +286,16 @@
 
             high, low = split(lax.fori_loop(0, TAPS, tap, jnp.zeros((LANES, LANES), F32)))
             for u in range(2):
-                rows = slice((u + 1 + shift) * LANES, (u + 2 + shift) * LANES)
-                h_hi[b, rows, u * LANES:(u + 1) * LANES] = high
-                h_lo[b, rows, u * LANES:(u + 1) * LANES] = low
+                for third, band in enumerate((high, high, low)):
+                    row = third * 2 * STEP + (u + 1 + shift) * LANES
+                    h_all[b, row:row + LANES, u * LANES:(u + 1) * LANES] = band
         return 0
 
     lax.fori_loop(0, NB, col_band, 0)
 
     for part_z in (z_hi, z_lo):
-        part_z[:, :, 0:LANES] = jnp.zeros((NB, PER * ROWS, LANES), BF16)
-        part_z[:, :, LANES + COLS:] = jnp.zeros((NB, PER * ROWS, LANES), BF16)
-
-    for d in range(1, N_EXP):
-        meta(d).wait_recv()
-    table = pltpu.make_async_copy(m_got, m_smem, own_s.at[1])
-    table.start()
-    table.wait()
+        part_z[:, :, 0:LANES] = jnp.zeros((NB, ROWS, LANES), BF16)
+        part_z[:, :, LANES + COLS:] = jnp.zeros((NB, ROWS, LANES), BF16)
 
     lane = iota((8, 2 * LANES), 1)
     lane_slot, lane_row = lane >> 3, lane & 7
@@ -287,7 +310,6 @@
         slots[p] = jnp.where(patch_row == target, 1.0, 0.0).astype(BF16)
         return 0
 
-    lax.fori_loop(0, N_SKY, select_rows, 0)
 
     def add_strips(got, acc, p):
         tiles = [
@@ -303,16 +325,32 @@
 
         return half
 
-    top, low_part = pl.ds(0, PR // 2), pl.ds(PR // 2, PR // 2)
-    w_z = Ring(NZ, z, at_z, lambda o: acc_w.at[o], halves(NX // 2), land_wz, wz_s, wz_r)
-    w_x = Ring(NX, x, at_x, lambda o: mid_w.at[o], halves(PR // 2), land_wx, wx_s, wx_r)
-    a_x = Ring(NX, x, at_x, lambda o: acc_v.at[:, o, top], halves(NZ // 2), land_ax, ax_s, ax_r)
-    a_z = Ring(NZ, z, at_z, lambda o: mid_a.at[o], halves(PR // 4), land_az, az_s, az_r)
-    b_z = Ring(NZ, z, at_z, lambda o: acc_v.at[o, :, low_part], halves(NX // 2), land_bz, bz_s, bz_r)
-    b_x = Ring(NX, x, at_x, lambda o: mid_b.at[o], halves(PR // 4), land_bx, bx_s, bx_r)
+    def sums(acc, rows, x_first, land, land2, mid, send, recv, send2, recv2):
+        if x_first:
+            ring = Ring(NX, x, at_x, lambda o: acc.at[:, o, rows], halves(NZ // 2), land, send, recv)
+            return ring, Direct(NZ, z, at_z, lambda o: mid.at[o], land2, send2, recv2)
+        ring = Ring(NZ, z, at_z, lambda o: acc.at[o, :, rows], halves(NX // 2), land, send, recv)
+        return ring, Direct(NX, x, at_x, lambda o: mid.at[o], land2, send2, recv2)
+
+    u_a, u_az = sums(acc_w, pl.ds(0, 64), True, land_ua, land_uaz, mid_ua, ua_s, ua_r, uaz_s, uaz_r)
+    u_b, u_bx = sums(acc_w, pl.ds(64, 64), False, land_ub, land_ubx, mid_ub, ub_s, ub_r, ubx_s, ubx_r)
+    a_x, a_z, b_z, b_x = [], [], [], []
+    for i in range(2):
+        first, second = sums(
+            acc_v, pl.ds(i * 32, 32), True, land_a.at[i], land_az.at[i], mid_a.at[i],
+            ax_s.at[i], ax_r.at[i], az_s.at[i], az_r.at[i],
+        )
+        a_x.append(first)
+        a_z.append(second)
+        first, second = sums(
+            acc_v, pl.ds(64 + i * 32, 32), False, land_b.at[i], land_bx.at[i], mid_b.at[i],
+            bz_s.at[i], bz_r.at[i], bx_s.at[i], bx_r.at[i],
+        )
+        b_z.append(first)
+        b_x.append(second)
 
     def send_v(c, d):
-        span = pl.ds(c * (8 * PER), 8 * PER)
+        span = pl.ds(c * (8 * SEND), 8 * SEND)
         return pltpu.make_async_remote_copy(
             src_ref=v_buf.at[peers[d], span], dst_ref=v_got.at[exp, span],
             send_sem=v_s.at[c, d], recv_sem=v_r.at[c, d],
@@ -322,81 +360,93 @@
     third = iota((NB * ROWS, STEP), 1) >= 160
     low_rows = iota((8, STEP), 0) < 4
 
-    def chunk(c, _):
-        @pl.when(c == CHUNKS - 1)
+    def exposure(e, _):
+        @pl.when(e == SLOTS_AT)
         def _():
             for d in range(1, N_EXP):
-                send_w(d).wait_recv()
+                meta(d).wait_recv()
+            table = pltpu.make_async_copy(m_got, m_smem, own_s.at[1])
+            table.start()
+            table.wait()
+            lax.fori_loop(0, N_SKY, select_rows, 0)
+
+        @pl.when(e == WEIGHTS_AT)
+        def _():
+            def arrived_w(c, _):
+                for d in range(1, N_EXP):
+                    send_w(c, d).wait_recv()
+                return 0
+
+            lax.fori_loop(0, CHUNKS, arrived_w, 0)
             own_w.wait()
 
             def add_weights(p, _):
                 add_strips(w_got, acc_w, p)
                 return 0
 
-            lax.fori_loop(0, N_SKY, add_weights, 0)
-            w_z.begin()
-
-        def vertical(el, _):
-            e = c * PER + el
-            halo(0, e).wait_recv()
-            halo(1, e).wait_recv()
-            table_row = coef_index[e]
-            bands = [coef_table[b, table_row] * v_base[b] for b in range(NB)]
-            high, low = split(jnp.concatenate(bands, 0))
-            left = jnp.where(third, low.astype(F32), high.astype(F32)).astype(BF16)
-            out_rows = pl.ds(pl.multiple_of(el * ROWS, ROWS), ROWS)
-            for j in range(NSTEP):
-                part, at = divmod(j * STEP, HALF)
-                cols = slice(at, at + STEP)
-                up = h_recv[0, e, 2 * part:2 * part + 2, :, cols].reshape(16, STEP)
-                down = h_recv[1, e, 2 * part:2 * part + 2, :, cols].reshape(16, STEP)
-                up4, down4 = h_recv[0, e, 4, :, cols], h_recv[1, e, 4, :, cols]
-                if part == 0:
-                    rest = jnp.where(low_rows, down4, up4)
-                else:
-                    rest = pltpu.roll(jnp.where(low_rows, up4, down4), 4, 0)
-                rows = jnp.concatenate(
-                    [image[e, :, j * STEP:(j + 1) * STEP], up, down, rest, jnp.zeros((8, STEP), F32)], 0
-                )
-                x_hi, x_lo = split(rows)
-                right = jnp.concatenate([x_hi, x_lo, x_hi, jnp.zeros((16, STEP), BF16)], 0)
-                high_z, low_z = split(jnp.dot(left, right, preferred_element_type=F32))
-                at = LANES + j * STEP
-                z_hi[:, out_rows, at:at + STEP] = high_z.reshape(NB, ROWS, STEP)
-                z_lo[:, out_rows, at:at + STEP] = low_z.reshape(NB, ROWS, STEP)
-            return 0
-
-        lax.fori_loop(0, PER, vertical, 0)
-
-        def horizontal(j, _):
-            cols = pl.ds(pl.multiple_of(j * STEP, STEP), 2 * STEP)
-            total = jnp.zeros((PER * ROWS, STEP), F32)
-            for b in range(NB):
-                zh, zl = z_hi[b, :, cols], z_lo[b, :, cols]
-                total += jnp.dot(zh, h_hi[b], preferred_element_type=F32)
-                total += jnp.dot(zl, h_hi[b], preferred_element_type=F32)
-                total += jnp.dot(zh, h_lo[b], preferred_element_type=F32)
+            lax.fori_loop(0, N_SKY, add_weights, 0, unroll=4)
+            u_b.begin()
+            u_a.begin()
+
+        halo(0, e).wait_recv()
+        halo(1, e).wait_recv()
+        table_row = coef_index[e]
+        bands = [coef_table[b, table_row] * v_base[b] for b in range(NB)]
+        high, low = split(jnp.concatenate(bands, 0))
+        left = jnp.where(third, low.astype(F32), high.astype(F32)).astype(BF16)
+        for j in range(NSTEP):
+            part, at = divmod(j * STEP, HALF)
+            cols = slice(at, at + STEP)
+            up = h_recv[0, e, 2 * part:2 * part + 2, :, cols].reshape(16, STEP)
+            down = h_recv[1, e, 2 * part:2 * part + 2, :, cols].reshape(16, STEP)
+            up4, down4 = h_recv[0, e, 4, :, cols], h_recv[1, e, 4, :, cols]
+            if part == 0:
+                rest = jnp.where(low_rows, down4, up4)
+            else:
+                rest = pltpu.roll(jnp.where(low_rows, up4, down4), 4, 0)
+            rows = jnp.concatenate(
+                [image[e, :, j * STEP:(j + 1) * STEP], up, down, rest, jnp.zeros((8, STEP), F32)], 0
+            )
+            x_hi, x_lo = split(rows)
+            right = jnp.concatenate([x_hi, x_lo, x_hi, jnp.zeros((16, STEP), BF16)], 0)
+            high_z, low_z = split(jnp.dot(left, right, preferred_element_type=F32))
+            at = LANES + j * STEP
+            z_hi[:, :, at:at + STEP] = high_z.reshape(NB, ROWS, STEP)
+            z_lo[:, :, at:at + STEP] = low_z.reshape(NB, ROWS, STEP)
+
+        total = jnp.zeros((NSTEP * ROWS, STEP), F32)
+        for b in range(NB):
+            highs = jnp.concatenate([z_hi[b, :, j * STEP:(j + 2) * STEP] for j in range(NSTEP)], 0)
+            lows = jnp.concatenate([z_lo[b, :, j * STEP:(j + 2) * STEP] for j in range(NSTEP)], 0)
+            total += jnp.dot(jnp.concatenate([highs, lows, highs], 1), h_all[b], preferred_element_type=F32)
+        for j in range(NSTEP):
             part = j // 4
             for u in range(2):
-                q = lax.rem(j, 4) * 2 + u
-                for r in range(4 * PER):
-                    piece = total[r * 8:(r + 1) * 8, u * LANES:(u + 1) * LANES]
-                    strip = (c * (4 * PER) + r) * 2 + part
-                    v_buf[q, strip] = piece * w_buf[q, strip]
-            return 0
-
-        lax.fori_loop(0, NSTEP, horizontal, 0)
-        for d in range(1, N_EXP):
-            send_v(c, d).start()
-        return 0
-
-    lax.fori_loop(0, CHUNKS, chunk, 0)
+                q = (j % 4) * 2 + u
+                for r in range(4):
+                    row = j * ROWS + r * 8
+                    strip = (e * 4 + r) * 2 + part
+                    v_buf[q, strip] = total[row:row + 8, u * LANES:(u + 1) * LANES] * w_buf[q, strip]
+
+        @pl.when(lax.rem(e, SEND) == SEND - 1)
+        def _():
+            for d in range(1, N_EXP):
+                send_v(e // SEND, d).start()
+
+        return 0
+
+    lax.fori_loop(0, EXPS, exposure, 0)
     own_v = pltpu.make_async_copy(v_buf.at[exp], v_got.at[exp], own_s.at[2])
     own_v.start()
 
-    w_z.advance(1)
-    w_z.advance(2)
-    w_z.advance(3)
+    u_b.advance(1)
+    u_a.advance(1)
+    u_b.advance(2)
+    mid_ua[...] = u_a.total()
+    u_az.begin()
+    u_b.advance(3)
+    mid_ub[...] = u_b.total()
+    u_bx.begin()
 
     def arrived_v(c, _):
         for d in range(1, N_EXP):
@@ -406,23 +456,28 @@
     lax.fori_loop(0, CHUNKS, arrived_v, 0)
     own_v.wait()
 
-    def add_values(p, _):
-        add_strips(v_got, acc_v, p)
-        return 0
-
-    lax.fori_loop(0, N_SKY, add_values, 0)
-    a_x.begin()
-    b_z.begin()
-    mid_w[...] = w_z.total()
-    w_x.begin()
-    a_x.advance(1)
-    b_z.advance(1)
-    w_x.advance(1)
-    b_z.advance(2)
-    mid_a[...] = a_x.total()
-    a_z.begin()
-    b_z.advance(3)
-    fin_w[...] = w_x.total()
+    def add_values(distance):
+        owner = lax.rem(z + distance, NZ)
+
+        def add(px, _):
+            add_strips(v_got, acc_v, owner * NX + px)
+            return 0
+
+        lax.fori_loop(0, NX, add, 0, unroll=True)
+
+    add_values(4)
+    for ring in b_z:
+        ring.begin(0)
+    add_values(3)
+    add_values(5)
+    for ring in b_z:
+        ring.begin(1)
+    for distance in (2, 6, 1, 7, 0):
+        add_values(distance)
+    for ring in a_x:
+        ring.begin()
+    fin_w[0:64] = u_az.total()
+    fin_w[64:128] = u_bx.total()
 
     def rows_copy(fin, land, send, recv, d):
         return pltpu.make_async_remote_copy(
@@ -436,14 +491,24 @@
     for d in range(1, N_EXP):
         rows_copy(fin_w, rows_w, rw_s, rw_r, d).start()
     rows_w[exp] = fin_w[mine]
-    a_z.advance(1)
-    mid_b[...] = b_z.total()
-    b_x.begin()
-    a_z.advance(2)
-    b_x.advance(1)
-    a_z.advance(3)
-    fin_v[PR // 2:] = b_x.total()
-    fin_v[:PR // 2] = a_z.total()
+    for ring in b_z:
+        ring.advance(1)
+    for ring in a_x:
+        ring.advance(1)
+    for ring in b_z:
+        ring.advance(2)
+    for i in range(2):
+        mid_a[i] = a_x[i].total()
+        a_z[i].begin()
+    for ring in b_z:
+        ring.advance(3)
+    for i in range(2):
+        mid_b[i] = b_z[i].total()
+        b_x[i].begin()
+    for i in range(2):
+        fin_v[i * 32:(i + 1) * 32] = a_z[i].total()
+    for i in range(2):
+        fin_v[64 + i * 32:96 + i * 32] = b_x[i].total()
     for d in range(1, N_EXP):
         rows_copy(fin_v, rows_v, rv_s, rv_r, d).start()
     rows_v[exp] = fin_v[mine]
@@ -460,15 +525,15 @@
     lax.fori_loop(0, EXPS, end_halo, 0)
     for d in range(1, N_EXP):
         meta(d).wait_send()
-        send_w(d).wait_send()
 
     def end_v(c, _):
         for d in range(1, N_EXP):
+            send_w(c, d).wait_send()
             send_v(c, d).wait_send()
         return 0
 
     lax.fori_loop(0, CHUNKS, end_v, 0)
-    for ring in (w_z, w_x, a_x, a_z, b_z, b_x):
+    for ring in (u_a, u_az, u_b, u_bx, *a_x, *a_z, *b_z, *b_x):
         ring.drain()
     for d in range(1, N_EXP):
         rows_copy(fin_v, rows_v, rv_s, rv_r, d).wait()
@@ -496,24 +561,28 @@
             held(8, LANES, dtype=I32), held(N_EXP, 8, LANES, dtype=I32),
             pltpu.SMEM((N_EXP, 8, LANES), I32),
             held(N_SKY, PR, 2 * LANES, dtype=BF16),
-            held(NB, PER * ROWS, COLS + 2 * LANES, dtype=BF16),
-            held(NB, PER * ROWS, COLS + 2 * LANES, dtype=BF16),
-            held(NB, 2 * STEP, STEP, dtype=BF16),
-            held(NB, 2 * STEP, STEP, dtype=BF16),
+            held(NB, ROWS, COLS + 2 * LANES, dtype=BF16),
+            held(NB, ROWS, COLS + 2 * LANES, dtype=BF16),
+            held(NB, 6 * STEP, STEP, dtype=BF16),
             held(NB, ROWS, STEP),
             held(NZ, NX, PR, LANES), held(NZ, NX, PR, LANES),
-            held(2, 4, NX, PR, LANES), held(2, 2, PR, LANES),
-            held(2, 2, NZ, PR // 2, LANES), held(2, 4, PR // 2, LANES),
-            held(2, 4, NX, PR // 2, LANES), held(2, 2, PR // 2, LANES),
-            held(NX, PR, LANES), held(NZ, PR // 2, LANES), held(NX, PR // 2, LANES),
+            held(2, 2, NZ, 64, LANES), held(NZ, 64, LANES),
+            held(2, 4, NX, 64, LANES), held(NX, 64, LANES),
+            held(2, 2, 2, NZ, 32, LANES), held(2, NZ, 32, LANES),
+            held(2, 2, 4, NX, 32, LANES), held(2, NX, 32, LANES),
+            held(NZ, 64, LANES), held(NX, 64, LANES), held(2, NZ, 32, LANES), held(2, NX, 32, LANES),
             held(PR, LANES), held(PR, LANES),
             held(N_EXP, PR // N_EXP, LANES), held(N_EXP, PR // N_EXP, LANES),
             dma((2,)), dma((2, EXPS)), dma((2, EXPS)),
-            dma((N_EXP,)), dma((N_EXP,)),
+            dma((CHUNKS, N_EXP)), dma((CHUNKS, N_EXP)),
             dma((CHUNKS, N_EXP)), dma((CHUNKS, N_EXP)),
             dma((N_EXP,)), dma((N_EXP,)),
             dma((3,)),
-        ] + [dma((2, n)) for n in (5, 5, 3, 3, 3, 3, 5, 5, 5, 5, 3, 3)] + [dma((N_EXP,))] * 4,
+        ] + [
+            dma(shape)
+            for shape in ((2, 3), (NZ,), (2, 5), (NX,), (2, 2, 3), (2, NZ), (2, 2, 5), (2, NX), (N_EXP,), (N_EXP,))
+            for _ in range(2)
+        ],
         compiler_params=pltpu.CompilerParams(
             collective_id=0, has_side_effects=True, vmem_limit_bytes=60 * 1024 * 1024
         ),

time: 103 us -> 99.1 us (0.962)
  Pallas kernels: 101 us -> 96.8 us
    pallas_call x1, Pallas kernels: 101 us -> 96.8 us  [per_device(): pl.pallas_call(coadd_kernel, out_shape=jax.ShapeDtypeStruct((2, PR // N_E...]
where the time goes in v3:
time: 99.1 us; the launch traced here: 99 us
  Pallas kernels  96.8 us (98%)
  other arithmetic  1.53 us (2%)
    pallas_call x1, Pallas kernels, per_device(): pl.pallas_call(coadd_kernel, out_shape=jax.ShapeDtypeStruct((2, PR // N_E...  96.8 us

profile of v3, /device:TPU:1, one launch (start us, length us, event | category | flops | bytes accessed | tf_op | source)
XLA Modules:
  0.0 99.0 jit_solution(1461190152140396794)
XLA Ops:
  0.6 96.8 %shard_map.95 = f32[2,16,1024]{2,1,0:T(8,128)} custom-call(f32[8,32,2048]{2,1,0:T(8,128)} %image_in.1, f32[8,32,2048]{2,1,0:T(8,128)} %variance_in.1, s32[1,64]{1,0:T(1,128)} %bitcast.9, s32[1,64]{1,0:T(1,128)} %bitcast.10, s32[8]{0:T(128)} %coef_index.1, f32[5,16]{1,0:T(8,128)} %bitcast.8, f32[5,41]{1,0:T(8,128)} %row_taps.1, f32[5,41]{1,0:T(8,128)} %col_taps.1), custom_call_target="tpu_custom_call" | custom-call | tf_op jit(solution)/shard_map/pallas_call | solution.py:552
  97.4 1.5 %bitcast_divide_fusion = (f32[16,1024]{1,0:T(8,128)}, f32[16,1024]{1,0:T(8,128)}) fusion(f32[2,16,1024]{2,1,0:T(8,128)} %shard_map.95), kind=kLoop, calls=%fused_computation | loop fusion | flops 32768 | bytes 262144 | tf_op jit(solution)/shard_map/div | solution.py:593

commit v4 on v3

--- a/solution.py
+++ b/solution.py
@@ -14,10 +14,12 @@
 BLOCKS = EXPS * ROWS // 8
 LANES = 128
 PR, PATCH_ROWS = 128, 4096
-SEND = 2
+SEND = 4
 CHUNKS = EXPS // SEND
 SLOTS_AT = 3
 WEIGHTS_AT = 6
+A_PARTS, A_ROWS = 1, 64
+B_PARTS, B_ROWS = 1, 64
 STEP = 256
 NSTEP = COLS // STEP
 
@@ -231,11 +233,9 @@
             device_id=(sky, peers[d]), device_id_type=MESH,
         )
 
-    def send_w(c, d):
-        span = pl.ds(c * (8 * SEND), 8 * SEND)
+    def send_w(d):
         return pltpu.make_async_remote_copy(
-            src_ref=w_buf.at[peers[d], span], dst_ref=w_got.at[exp, span],
-            send_sem=w_s.at[c, d], recv_sem=w_r.at[c, d],
+            src_ref=w_buf.at[peers[d]], dst_ref=w_got.at[exp], send_sem=w_s.at[d], recv_sem=w_r.at[d],
             device_id=(sky, peers[d]), device_id_type=MESH,
         )
 
@@ -243,15 +243,15 @@
         meta(d).start()
     m_got[exp] = m_buf[...]
 
-    def start_sends(c, _):
-        for i in range(SEND):
-            halo(0, c * SEND + i).start()
-            halo(1, c * SEND + i).start()
-        for d in range(1, N_EXP):
-            send_w(c, d).start()
-        return 0
-
-    lax.fori_loop(0, CHUNKS, start_sends, 0)
+    for d in range(1, N_EXP):
+        send_w(d).start()
+
+    def start_halo(e, _):
+        halo(0, e).start()
+        halo(1, e).start()
+        return 0
+
+    lax.fori_loop(0, EXPS, start_halo, 0)
     own_w = pltpu.make_async_copy(w_buf.at[exp], w_got.at[exp], own_s.at[0])
     own_w.start()
 
@@ -335,19 +335,23 @@
     u_a, u_az = sums(acc_w, pl.ds(0, 64), True, land_ua, land_uaz, mid_ua, ua_s, ua_r, uaz_s, uaz_r)
     u_b, u_bx = sums(acc_w, pl.ds(64, 64), False, land_ub, land_ubx, mid_ub, ub_s, ub_r, ubx_s, ubx_r)
     a_x, a_z, b_z, b_x = [], [], [], []
-    for i in range(2):
-        first, second = sums(
-            acc_v, pl.ds(i * 32, 32), True, land_a.at[i], land_az.at[i], mid_a.at[i],
-            ax_s.at[i], ax_r.at[i], az_s.at[i], az_r.at[i],
-        )
-        a_x.append(first)
-        a_z.append(second)
-        first, second = sums(
-            acc_v, pl.ds(64 + i * 32, 32), False, land_b.at[i], land_bx.at[i], mid_b.at[i],
-            bz_s.at[i], bz_r.at[i], bx_s.at[i], bx_r.at[i],
-        )
-        b_z.append(first)
-        b_x.append(second)
+    for i in range(A_PARTS):
+        rows = pl.ds(i * A_ROWS, A_ROWS)
+        a_x.append(Ring(
+            NX, x, at_x, lambda o, rows=rows: acc_v.at[:, o, rows], halves(NZ // 2),
+            land_a.at[i], ax_s.at[i], ax_r.at[i],
+        ))
+        a_z.append(Ring(
+            NZ, z, at_z, lambda o, i=i: mid_a.at[i, o], halves(A_ROWS // 2),
+            land_az.at[i], az_s.at[i], az_r.at[i],
+        ))
+    for i in range(B_PARTS):
+        rows = pl.ds(A_PARTS * A_ROWS + i * B_ROWS, B_ROWS)
+        b_z.append(Ring(
+            NZ, z, at_z, lambda o, rows=rows: acc_v.at[o, :, rows], halves(NX // 2),
+            land_b.at[i], bz_s.at[i], bz_r.at[i],
+        ))
+        b_x.append(Direct(NX, x, at_x, lambda o, i=i: mid_b.at[i, o], land_bx.at[i], bx_s.at[i], bx_r.at[i]))
 
     def send_v(c, d):
         span = pl.ds(c * (8 * SEND), 8 * SEND)
@@ -372,13 +376,16 @@
 
         @pl.when(e == WEIGHTS_AT)
         def _():
-            def arrived_w(c, _):
+            for d in range(1, N_EXP):
+                send_w(d).wait_recv()
+            own_w.wait()
+
+            def send_held(c, _):
                 for d in range(1, N_EXP):
-                    send_w(c, d).wait_recv()
+                    send_v(c, d).start()
                 return 0
 
-            lax.fori_loop(0, CHUNKS, arrived_w, 0)
-            own_w.wait()
+            lax.fori_loop(0, WEIGHTS_AT // SEND, send_held, 0)
 
             def add_weights(p, _):
                 add_strips(w_got, acc_w, p)
@@ -428,7 +435,7 @@
                     strip = (e * 4 + r) * 2 + part
                     v_buf[q, strip] = total[row:row + 8, u * LANES:(u + 1) * LANES] * w_buf[q, strip]
 
-        @pl.when(lax.rem(e, SEND) == SEND - 1)
+        @pl.when((lax.rem(e, SEND) == SEND - 1) & (e >= WEIGHTS_AT))
         def _():
             for d in range(1, N_EXP):
                 send_v(e // SEND, d).start()
@@ -497,18 +504,24 @@
         ring.advance(1)
     for ring in b_z:
         ring.advance(2)
-    for i in range(2):
+    for i in range(A_PARTS):
         mid_a[i] = a_x[i].total()
         a_z[i].begin()
     for ring in b_z:
         ring.advance(3)
-    for i in range(2):
+    for ring in a_z:
+        ring.advance(1)
+    for i in range(B_PARTS):
         mid_b[i] = b_z[i].total()
         b_x[i].begin()
-    for i in range(2):
-        fin_v[i * 32:(i + 1) * 32] = a_z[i].total()
-    for i in range(2):
-        fin_v[64 + i * 32:96 + i * 32] = b_x[i].total()
+    for step in (2, 3):
+        for ring in a_z:
+            ring.advance(step)
+    for i in range(B_PARTS):
+        row = A_PARTS * A_ROWS + i * B_ROWS
+        fin_v[row:row + B_ROWS] = b_x[i].total()
+    for i in range(A_PARTS):
+        fin_v[i * A_ROWS:(i + 1) * A_ROWS] = a_z[i].total()
     for d in range(1, N_EXP):
         rows_copy(fin_v, rows_v, rv_s, rv_r, d).start()
     rows_v[exp] = fin_v[mine]
@@ -525,10 +538,10 @@
     lax.fori_loop(0, EXPS, end_halo, 0)
     for d in range(1, N_EXP):
         meta(d).wait_send()
+        send_w(d).wait_send()
 
     def end_v(c, _):
         for d in range(1, N_EXP):
-            send_w(c, d).wait_send()
             send_v(c, d).wait_send()
         return 0
 
@@ -568,19 +581,19 @@
             held(NZ, NX, PR, LANES), held(NZ, NX, PR, LANES),
             held(2, 2, NZ, 64, LANES), held(NZ, 64, LANES),
             held(2, 4, NX, 64, LANES), held(NX, 64, LANES),
-            held(2, 2, 2, NZ, 32, LANES), held(2, NZ, 32, LANES),
-            held(2, 2, 4, NX, 32, LANES), held(2, NX, 32, LANES),
-            held(NZ, 64, LANES), held(NX, 64, LANES), held(2, NZ, 32, LANES), held(2, NX, 32, LANES),
+            held(A_PARTS, 2, 2, NZ, A_ROWS, LANES), held(A_PARTS, 2, 4, A_ROWS, LANES),
+            held(B_PARTS, 2, 4, NX, B_ROWS, LANES), held(B_PARTS, NX, B_ROWS, LANES),
+            held(NZ, 64, LANES), held(NX, 64, LANES), held(A_PARTS, NZ, A_ROWS, LANES), held(B_PARTS, NX, B_ROWS, LANES),
             held(PR, LANES), held(PR, LANES),
             held(N_EXP, PR // N_EXP, LANES), held(N_EXP, PR // N_EXP, LANES),
             dma((2,)), dma((2, EXPS)), dma((2, EXPS)),
-            dma((CHUNKS, N_EXP)), dma((CHUNKS, N_EXP)),
+            dma((N_EXP,)), dma((N_EXP,)),
             dma((CHUNKS, N_EXP)), dma((CHUNKS, N_EXP)),
             dma((N_EXP,)), dma((N_EXP,)),
             dma((3,)),
         ] + [
             dma(shape)
-            for shape in ((2, 3), (NZ,), (2, 5), (NX,), (2, 2, 3), (2, NZ), (2, 2, 5), (2, NX), (N_EXP,), (N_EXP,))
+            for shape in ((2, 3), (NZ,), (2, 5), (NX,), (A_PARTS, 2, 3), (A_PARTS, 2, 5), (B_PARTS, 2, 5), (B_PARTS, NX), (N_EXP,), (N_EXP,))
             for _ in range(2)
         ],
         compiler_params=pltpu.CompilerParams(

time: 99.1 us -> 96.4 us (0.973)
  Pallas kernels: 96.8 us -> 94 us
    pallas_call x1, Pallas kernels: 96.8 us -> 94 us  [per_device(): pl.pallas_call(coadd_kernel, out_shape=jax.ShapeDtypeStruct((2, PR // N_E...]
where the time goes in v4:
time: 96.4 us; the launch traced here: 96.2 us
  Pallas kernels  94 us (98%)
  other arithmetic  1.53 us (2%)
    pallas_call x1, Pallas kernels, per_device(): pl.pallas_call(coadd_kernel, out_shape=jax.ShapeDtypeStruct((2, PR // N_E...  94 us

profile of v4, /device:TPU:1, one launch (start us, length us, event | category | flops | bytes accessed | tf_op | source)
XLA Modules:
  0.0 96.2 jit_solution(4208500721779741035)
XLA Ops:
  0.6 94.0 %shard_map.95 = f32[2,16,1024]{2,1,0:T(8,128)} custom-call(f32[8,32,2048]{2,1,0:T(8,128)} %image_in.1, f32[8,32,2048]{2,1,0:T(8,128)} %variance_in.1, s32[1,64]{1,0:T(1,128)} %bitcast.9, s32[1,64]{1,0:T(1,128)} %bitcast.10, s32[8]{0:T(128)} %coef_index.1, f32[5,16]{1,0:T(8,128)} %bitcast.8, f32[5,41]{1,0:T(8,128)} %row_taps.1, f32[5,41]{1,0:T(8,128)} %col_taps.1), custom_call_target="tpu_custom_call" | custom-call | tf_op jit(solution)/shard_map/pallas_call | solution.py:565
  94.7 1.5 %bitcast_divide_fusion = (f32[16,1024]{1,0:T(8,128)}, f32[16,1024]{1,0:T(8,128)}) fusion(f32[2,16,1024]{2,1,0:T(8,128)} %shard_map.95), kind=kLoop, calls=%fused_computation | loop fusion | flops 32768 | bytes 262144 | tf_op jit(solution)/shard_map/div | solution.py:606

commit v5 on v4

--- a/solution.py
+++ b/solution.py
@@ -17,6 +17,7 @@
 SEND = 4
 CHUNKS = EXPS // SEND
 SLOTS_AT = 3
+RELEASE_AT = 5
 WEIGHTS_AT = 6
 A_PARTS, A_ROWS = 1, 64
 B_PARTS, B_ROWS = 1, 64
@@ -380,12 +381,6 @@
                 send_w(d).wait_recv()
             own_w.wait()
 
-            def send_held(c, _):
-                for d in range(1, N_EXP):
-                    send_v(c, d).start()
-                return 0
-
-            lax.fori_loop(0, WEIGHTS_AT // SEND, send_held, 0)
 
             def add_weights(p, _):
                 add_strips(w_got, acc_w, p)
@@ -435,10 +430,15 @@
                     strip = (e * 4 + r) * 2 + part
                     v_buf[q, strip] = total[row:row + 8, u * LANES:(u + 1) * LANES] * w_buf[q, strip]
 
-        @pl.when((lax.rem(e, SEND) == SEND - 1) & (e >= WEIGHTS_AT))
+        @pl.when(e == RELEASE_AT)
         def _():
             for d in range(1, N_EXP):
-                send_v(e // SEND, d).start()
+                send_v(0, d).start()
+
+        @pl.when(e == EXPS - 1)
+        def _():
+            for d in range(1, N_EXP):
+                send_v(1, d).start()
 
         return 0
 

time: 96.4 us -> 94.9 us (0.984)
  Pallas kernels: 94 us -> 92.6 us
    pallas_call x1, Pallas kernels: 94 us -> 92.6 us  [per_device(): pl.pallas_call(coadd_kernel, out_shape=jax.ShapeDtypeStruct((2, PR // N_E...]
where the time goes in v5:
time: 94.9 us; the launch traced here: 94.7 us
  Pallas kernels  92.6 us (98%)
  other arithmetic  1.53 us (2%)
    pallas_call x1, Pallas kernels, per_device(): pl.pallas_call(coadd_kernel, out_shape=jax.ShapeDtypeStruct((2, PR // N_E...  92.6 us

profile of v5, /device:TPU:1, one launch (start us, length us, event | category | flops | bytes accessed | tf_op | source)
XLA Modules:
  0.0 94.7 jit_solution(15593866589916149443)
XLA Ops:
  0.6 92.6 %shard_map.95 = f32[2,16,1024]{2,1,0:T(8,128)} custom-call(f32[8,32,2048]{2,1,0:T(8,128)} %image_in.1, f32[8,32,2048]{2,1,0:T(8,128)} %variance_in.1, s32[1,64]{1,0:T(1,128)} %bitcast.9, s32[1,64]{1,0:T(1,128)} %bitcast.10, s32[8]{0:T(128)} %coef_index.1, f32[5,16]{1,0:T(8,128)} %bitcast.8, f32[5,41]{1,0:T(8,128)} %row_taps.1, f32[5,41]{1,0:T(8,128)} %col_taps.1), custom_call_target="tpu_custom_call" | custom-call | tf_op jit(solution)/shard_map/pallas_call | solution.py:565
  93.2 1.5 %bitcast_divide_fusion = (f32[16,1024]{1,0:T(8,128)}, f32[16,1024]{1,0:T(8,128)}) fusion(f32[2,16,1024]{2,1,0:T(8,128)} %shard_map.95), kind=kLoop, calls=%fused_computation | loop fusion | flops 32768 | bytes 262144 | tf_op jit(solution)/shard_map/div | solution.py:606
